TPU v7x, 512 devices: a whole 4x4x16 slice. The times are simulated.
512 devices in a mesh: member: 16 (over z), space: 32 (over x, y, core).
Axes of the slice: x: 4, y: 4, z: 16, core: 2. Of those that a mesh axis runs over, the one named last changes fastest.
Arguments:
- background_samples: float32 [80, 524288], P('member', 'space'), may hold values from -6 to 6
- measured_quantity: float32 [2, 32768], P(None, 'space'), may hold values from -6 to 6
- measurement_noise_variance: float32 [2, 32768], P(None, 'space'), may hold values from 0.25 to 2
- measured_grid_point: int32 [2, 32768], P(None, 'space'), may hold values from 0 to 16383
- measurement_sort: int32 [2, 32768], P(None, 'space'), may hold values from 0 to 3
- distance_damping_weights: float32 [4, 8], replicated, may hold values from 0.2 to 1
Outputs:
- analysis: float32 [80, 524288], P('member', 'space')
Inputs may be any that keep to these rules, and one draw needn't show every extreme that they name: Observation j of a batch is owned by block j // 1024; measured_grid_point counts cells inside that block.
All inputs are finite; a program needn't handle non-finite values.
Results may differ from a plain program's by a relative error of at most 0.0003.
Values sent between devices are 32-bit elements; how exact they have to be, the bound alone decides.
No kernel may reach another device: no remote copies, remote signals or barrier semaphores. Data moves between devices by JAX's collectives and lax.ppermute only.
A program may use at most 128 MiB of HBM per device.

v0:
```python
import jax
import jax.numpy as jnp
from jax import lax
from jax.experimental import pallas as pl
from jax.experimental.pallas import tpu as pltpu
from jax.sharding import PartitionSpec as P

MEMBERS = 80
CELLS = 1024
BLOCK = 16384
BIN_BITS = 11
BINS = 8
CLASSES = 4
ROWS = 640
BUNDLE = 672
TILE = 256
TILES = 12
f32 = jnp.float32
bf16 = jnp.bfloat16
VM = pl.BlockSpec(memory_space=pltpu.VMEM)
SM = pl.BlockSpec(memory_space=pltpu.SMEM)
PARAMS = pltpu.CompilerParams(vmem_limit_bytes=48 * 1024 * 1024)


def split(value):
    high = value.astype(bf16)
    low = (value - high.astype(f32)).astype(bf16)
    return high, low


def pick_kernel(x_ref, gp_ref, send_ref, picks_ref, parts_ref):
    for c in range(128):
        d, r = c // 8, c % 8
        slab = x_ref[:, c * 128 : (c + 1) * 128]
        send_ref[pl.ds(d * 40 + r, 5, stride=8), :] = slab
    lane = lax.broadcasted_iota(jnp.int32, (128, 128), 0)
    for m in range(5):
        slabs = jnp.concatenate([send_ref[d * 40 + m * 8 : d * 40 + m * 8 + 8, :] for d in range(16)], axis=0)
        high, low = split(slabs)
        parts_ref[m * 128 : (m + 1) * 128, :128] = high
        parts_ref[m * 128 : (m + 1) * 128, 128:] = low
    for b in range(2):
        for r in range(8):
            cell = gp_ref[b : b + 1, r * 128 : (r + 1) * 128]
            onehot = jnp.where((cell & 127) == lane, 1.0, 0.0).astype(bf16)
            found = jnp.dot(
                parts_ref[...], jnp.concatenate([onehot, onehot], axis=0), preferred_element_type=f32
            )
            here = lane == (cell >> 7)
            for m in range(5):
                value = jnp.where(here, found[m * 128 : (m + 1) * 128, :], 0.0)
                picks_ref[b * 40 + m * 8 + r : b * 40 + m * 8 + r + 1, :] = jnp.sum(value, axis=0, keepdims=True)


def pick(samples, grid_point):
    return pl.pallas_call(
        pick_kernel,
        out_shape=(jax.ShapeDtypeStruct((ROWS, 128), f32), jax.ShapeDtypeStruct((80, 128), f32)),
        in_specs=[VM, VM],
        out_specs=(VM, VM),
        scratch_shapes=[pltpu.VMEM((640, 256), bf16)],
        compiler_params=PARAMS,
        name="pick",
    )(samples, grid_point)


def bundle_kernel(gathered_ref, par_ref, bundle_ref, cells_ref):
    for k in range(16):
        bundle_ref[k * 40 : (k + 1) * 40, :] = gathered_ref[k * 80 : k * 80 + 40, :]
        cells_ref[k * 40 : (k + 1) * 40, :] = gathered_ref[k * 80 + 40 : k * 80 + 80, :]
    bundle_ref[ROWS:BUNDLE, :] = par_ref[...]


def make_bundle(gathered, par):
    return pl.pallas_call(
        bundle_kernel,
        out_shape=(jax.ShapeDtypeStruct((BUNDLE, 128), f32), jax.ShapeDtypeStruct((ROWS, 128), f32)),
        in_specs=[VM, VM],
        out_specs=(VM, VM),
        compiler_params=PARAMS,
        name="bundle",
    )(gathered, par)


def taper_of(classes, tab_ref):
    rows = []
    for b in range(BINS):
        row = jnp.zeros(classes.shape, f32)
        for c in range(CLASSES):
            row = jnp.where(classes == c, tab_ref[c, b], row)
        rows.append(row)
    return rows


def prepare_section(sec, ref, where, tab_ref, d3_ref, a2_ref, rows_ref, bulk):
    place = ref[656:664, :].astype(jnp.int32)
    classes = ref[664:672, :].astype(jnp.int32)
    taper = taper_of(classes, tab_ref)
    if bulk:
        first = where - place
        rising = first >= 0
        dist = jnp.abs(first)
        bin0 = dist >> BIN_BITS
        inner = dist & ((1 << BIN_BITS) - 1)
        turn = jnp.where(rising, (1 << BIN_BITS) - inner, inner + 1)
        bin1 = jnp.where(rising, bin0 + 1, jnp.maximum(bin0 - 1, 0))
        before = jnp.zeros(classes.shape, f32)
        after = jnp.zeros(classes.shape, f32)
        for b in range(BINS):
            before = jnp.where(bin0 == b, taper[b], before)
            after = jnp.where(bin1 == b, taper[b], after)
    else:
        shifted = place - where
    for r in range(8):
        tile, col = (sec * 8 + r) // 2, ((sec * 8 + r) % 2) * 128
        cols = slice(col, col + 128)
        prior = ref[pl.ds(r, MEMBERS, stride=8), :]
        mean = jnp.sum(prior, axis=0, keepdims=True) / MEMBERS
        dev = prior - mean
        spread = jnp.sum(dev * dev, axis=0, keepdims=True) / (MEMBERS - 1)
        value = ref[640 + r : 641 + r, :]
        error = ref[648 + r : 649 + r, :]
        total = spread + error
        scale = 1.0 / (total * (MEMBERS - 1))
        shrink = 1.0 / (1.0 + jnp.sqrt(error / total))
        step = (value - mean) - shrink * dev
        high, low = split(dev)
        d3_ref[tile, 0:80, cols] = high
        d3_ref[tile, 80:160, cols] = high
        d3_ref[tile, 160:240, cols] = low
        d3_ref[tile, 240:256, cols] = jnp.zeros((16, 128), bf16)
        high, low = split(step)
        pad = jnp.zeros((48, 128), bf16)
        a2_ref[tile, 0:80, cols] = high
        a2_ref[tile, 80:128, cols] = pad
        a2_ref[tile, 128:208, cols] = low
        a2_ref[tile, 208:256, cols] = pad
        full = (8, 128)
        if bulk:
            rows_ref[tile, 0:8, cols] = jnp.broadcast_to(turn[r : r + 1, :].astype(f32), full)
            rows_ref[tile, 8:16, cols] = jnp.broadcast_to(before[r : r + 1, :] * scale, full)
            rows_ref[tile, 16:24, cols] = jnp.broadcast_to(after[r : r + 1, :] * scale, full)
        else:
            rows_ref[tile, 0:8, cols] = jnp.broadcast_to(shifted[r : r + 1, :].astype(f32), full)
            table = jnp.concatenate([taper[b][r : r + 1, :] * scale for b in range(BINS)], axis=0)
            rows_ref[tile, 8:16, cols] = table


def update_kernel(
    bulk, at_ref, tab_ref, x_ref, pos_ref, own_ref, side_ref, off_ref, out_ref, e3_ref, d3_ref, a2_ref, rows_ref, acc_ref, posb_ref
):
    start = at_ref[0] if bulk else 0
    for r in range(8):
        cells = x_ref[pl.ds(r, MEMBERS, stride=8), :]
        dev = cells - jnp.sum(cells, axis=0, keepdims=True) / MEMBERS
        high = dev.astype(bf16).astype(f32)
        low = dev - high
        stacked = jnp.concatenate([high, low, high, jnp.zeros((16, 128), f32)], axis=0)
        e3_ref[r * 128 : (r + 1) * 128, :] = stacked.T.astype(bf16)
        if not bulk:
            row = jnp.broadcast_to(pos_ref[r : r + 1, :], (128, 128))
            posb_ref[r * 128 : (r + 1) * 128, :] = row.T
    for sec, (ref, offset) in enumerate(((own_ref, 0), (side_ref, at_ref[1]), (off_ref, at_ref[2]))):
        prepare_section(sec, ref, start - offset, tab_ref, d3_ref, a2_ref, rows_ref, bulk)
    acc_ref[...] = jnp.zeros_like(acc_ref)
    part = 256

    def tile_step(tile, carry):
        for ic in range(CELLS // part):
            rows = slice(ic * part, (ic + 1) * part)
            cov = jnp.dot(e3_ref[rows, :], d3_ref[tile], preferred_element_type=f32)
            cov = cov.reshape(part // 8, 8, TILE)
            if bulk:
                at = lax.broadcasted_iota(jnp.int32, (part, TILE), 0).astype(f32).reshape(part // 8, 8, TILE) + float(ic * part)
                turn = rows_ref[tile, 0:8, :][None]
                weight = jnp.where(at >= turn, rows_ref[tile, 16:24, :][None], rows_ref[tile, 8:16, :][None])
            else:
                halves = []
                for h in range(2):
                    cols = slice(h * 128, (h + 1) * 128)
                    place = rows_ref[tile, 0:8, cols]
                    table = rows_ref[tile, 8:16, cols]
                    slabs = []
                    for g in range(part // 8):
                        pos = posb_ref[ic * part + g * 8 : ic * part + g * 8 + 8, :]
                        dist = jnp.abs(pos - place).astype(jnp.int32)
                        level = dist >> BIN_BITS
                        got = jnp.take_along_axis(table, level & (BINS - 1), axis=0, mode="promise_in_bounds")
                        slabs.append(jnp.where(level < BINS, got, 0.0)[None])
                    halves.append(jnp.concatenate(slabs, axis=0))
                weight = jnp.concatenate(halves, axis=2)
            gain = (weight * cov).reshape(part, TILE)
            high, low = split(gain)
            nt = (((1,), (1,)), ((), ()))
            acc_ref[rows, :] += lax.dot_general(high, a2_ref[tile], nt, preferred_element_type=f32)
            acc_ref[rows, :128] += lax.dot_general(low, a2_ref[tile, 0:128, :], nt, preferred_element_type=f32)
        return carry

    lax.fori_loop(0, TILES, tile_step, 0)
    for r in range(8):
        rows = slice(r * 128, (r + 1) * 128)
        step = (acc_ref[rows, :128] + acc_ref[rows, 128:]).T
        out_ref[pl.ds(r, MEMBERS, stride=8), :] = x_ref[pl.ds(r, MEMBERS, stride=8), :] + step[:MEMBERS, :]


def update(bulk, at, tab, x, pos, own, side, off):
    def kernel(*refs):
        update_kernel(bulk, *refs)

    return pl.pallas_call(
        kernel,
        out_shape=jax.ShapeDtypeStruct((ROWS, 128), f32),
        in_specs=[SM, SM, VM, VM, VM, VM, VM],
        out_specs=VM,
        scratch_shapes=[
            pltpu.VMEM((CELLS, 256), bf16),
            pltpu.VMEM((TILES, 256, TILE), bf16),
            pltpu.VMEM((TILES, 256, TILE), bf16),
            pltpu.VMEM((TILES, 24, TILE), f32),
            pltpu.VMEM((CELLS, 256), f32),
            pltpu.VMEM((CELLS, 128), f32),
        ],
        compiler_params=PARAMS,
        cost_estimate=pl.CostEstimate(flops=6_000_000_000, bytes_accessed=2_000_000, transcendentals=0),
        name="update_cells" if bulk else "update_obs",
    )(at, tab, x, pos, own, side, off)


def unsend_kernel(x_ref, out_ref):
    for c in range(128):
        d, r = c // 8, c % 8
        out_ref[:, c * 128 : (c + 1) * 128] = x_ref[pl.ds(d * 40 + r, 5, stride=8), :]


def unsend(x):
    return pl.pallas_call(
        unsend_kernel,
        out_shape=jax.ShapeDtypeStruct((5, BLOCK), f32),
        in_specs=[VM],
        out_specs=VM,
        compiler_params=PARAMS,
        name="unsend",
    )(x)


def per_device(samples, quantity, variance, grid_point, sort, tab):
    count = lax.axis_size("space")
    space = lax.axis_index("space")
    member = lax.axis_index("member")
    swap = [(i, i ^ 1) for i in range(count)]
    hop = [(i, (i + (1 if i % 2 else -1)) % count) for i in range(count)]
    sign = jnp.where(space % 2 == 0, BLOCK, -BLOCK)
    at = jnp.stack([member * CELLS, sign, -sign]).astype(jnp.int32)
    par = jnp.stack([quantity, variance, grid_point.astype(f32), sort.astype(f32)], axis=1).reshape(2, 32, 128)

    send, picks = pick(samples, grid_point)
    gathered = lax.all_gather(picks, "member", axis=0).reshape(2 * ROWS, 128)
    cells = lax.all_to_all(send.reshape(16, 40, 128), "member", 0, 0, tiled=True).reshape(ROWS, 128)
    own, second = make_bundle(gathered, par[0])
    side = lax.ppermute(own, "space", swap)
    off = lax.ppermute(own, "space", hop)
    pos = par[1, 16:24]
    second = update(False, at, tab, second, pos, own, side, off)
    own2 = jnp.concatenate([second, par[1]], axis=0)
    side2 = lax.ppermute(own2, "space", swap)
    off2 = lax.ppermute(own2, "space", hop)
    cells = update(True, at, tab, cells, pos, own, side, off)
    cells = update(True, at, tab, cells, pos, own2, side2, off2)
    back = lax.all_to_all(cells.reshape(16, 5, 8, 128)
                          .reshape(ROWS, 128).reshape(16, 40, 128), "member", 0, 0, tiled=True)
    return unsend(back.reshape(ROWS, 128))


def solution(mesh):
    in_specs = (
        P("member", "space"),
        P(None, "space"),
        P(None, "space"),
        P(None, "space"),
        P(None, "space"),
        P(),
    )
    return jax.shard_map(
        per_device, mesh=mesh, in_specs=in_specs, out_specs=P("member", "space"), check_vma=False
    )
```

profile of v0, /device:TPU:24, one launch (start us, length us, event | category | flops | bytes accessed | tf_op | source)
XLA Modules:
  0.0 152.9 jit_solution(4304886086815429452)
XLA Ops:
  0.0 1.0 copy-done
  1.0 0.7 copy-done.1
  1.7 1.6 %pick.1 = (f32[640,128]{1,0:T(8,128)}, f32[80,128]{1,0:T(8,128)S(1)}) custom-call(f32[5,16384]{1,0:T(8,128)S(1)} %copy-done, s32[2,1024]{1,0:T(2,128)S(1)} %copy-done.1), custom_call_target="tpu_custom_call" | custom-call | tf_op jit(solution)/shard_map/pick/pallas_call | solution.py:56
  3.4 0.0 copy-start.2
  3.4 15.2 %all-to-all-start = ((f32[16,40,128]{2,1,0:T(8,128)}), f32[16,40,128]{2,1,0:T(8,128)S(1)}, u32[]{:S(2)}, u32[]{:S(2)}) async-start(f32[16,40,128]{2,1,0:T(8,128)} %bitcast.3), calls=%async_computation | async-start | bytes 655360 | tf_op jit(solution)/shard_map/all_to_all | solution.py:258
  18.6 0.0 copy-start.4
  18.6 0.7 copy-done.4
  19.3 43.1 %all-gather.gathered_ref = f32[1280,128]{1,0:T(8,128)S(1)} all-gather(f32[80,128]{1,0:T(8,128)S(1)} %get-tuple-element.10), channel_id=2, replica_groups=mesh['member'=16,'space'=32] {'member'}, dimensions={0}, use_global_device_ids=true | all-gather | bytes 696320 | tf_op jit(solution)/shard_map/all_gather | solution.py:257
  62.5 0.0 copy-done.6
  62.6 1.9 %collective-permute-start.1 = (f32[672,128]{1,0:T(8,128)S(1)}, f32[672,128]{1,0:T(8,128)S(1)}, u32[]{:S(2)}, u32[]{:S(2)}) collective-permute-start(f32[672,128]{1,0:T(8,128)S(1)} %get-tuple-element.11.refs_4_), channel_id=1, source_target_pairs={{0,31},{1,2},{2,1},{3,4},{4,3},{5,6},{6,5},{7,8},{8,7},{9,10},{10,... | collective-permute-start | bytes 1032200 | tf_op jit(solution)/shard_map/ppermute | solution.py:261
  64.5 3.2 %collective-permute-start = (f32[672,128]{1,0:T(8,128)S(1)}, f32[672,128]{1,0:T(8,128)S(1)}, u32[]{:S(2)}, u32[]{:S(2)}) collective-permute-start(f32[672,128]{1,0:T(8,128)S(1)} %get-tuple-element.11.refs_4_), channel_id=1, source_target_pairs={{0,1},{1,0},{2,3},{3,2},{4,5},{5,4},{6,7},{7,6},{8,9},{9,8},{10,11... | collective-permute-start | bytes 1032200 | tf_op jit(solution)/shard_map/ppermute | solution.py:260
  67.8 0.1 pad_add_fusion.refs_0_
  67.8 3.3 %collective-permute-done.1.refs_6_ = f32[672,128]{1,0:T(8,128)S(1)} collective-permute-done((f32[672,128]{1,0:T(8,128)S(1)}, f32[672,128]{1,0:T(8,128)S(1)}, u32[]{:S(2)}, u32[]{:S(2)}) %collective-permute-start.1) | collective-permute-done | bytes 344096 | tf_op jit(solution)/shard_map/ppermute | solution.py:261
  71.1 0.0 collective-permute-done.refs_5_
  71.1 14.4 %update_obs.1 = f32[640,128]{1,0:T(8,128)S(1)} custom-call(s32[3]{0:T(128)S(1)} %pad_add_fusion.refs_0_, f32[4,8]{1,0:T(4,128)S(1)} %copy-done.3, f32[640,128]{1,0:T(8,128)S(1)} %get-tuple-element.12.refs_2_, f32[8,128]{1,0:T(8,128)S(1)} %slice_bitcast_fusion.refs_3_, f32[672,128]{1,0:T(8,128)S(1)} %get-tuple-element.11.refs_4_, ...), custom_call_target="tpu_custom_call" | custom-call | flops 6000000000 | bytes 2000000 | tf_op jit(solution)/shard_map/update_obs/pallas_call | solution.py:210
  85.6 2.2 %collective-permute-start.3 = (f32[672,128]{1,0:T(8,128)S(1)}, f32[672,128]{1,0:T(8,128)S(1)}, u32[]{:S(2)}, u32[]{:S(2)}) collective-permute-start(f32[672,128]{1,0:T(8,128)S(1)} %pad_maximum_fusion.refs_4_), channel_id=1, source_target_pairs={{0,31},{1,2},{2,1},{3,4},{4,3},{5,6},{6,5},{7,8},{8,7},{9,10},{10,... | collective-permute-start | bytes 1032200 | tf_op jit(solution)/shard_map/ppermute | solution.py:266
  87.8 5.0 %collective-permute-start.2 = (f32[672,128]{1,0:T(8,128)S(1)}, f32[672,128]{1,0:T(8,128)S(1)}, u32[]{:S(2)}, u32[]{:S(2)}) collective-permute-start(f32[672,128]{1,0:T(8,128)S(1)} %pad_maximum_fusion.refs_4_), channel_id=1, source_target_pairs={{0,1},{1,0},{2,3},{3,2},{4,5},{5,4},{6,7},{7,6},{8,9},{9,8},{10,11... | collective-permute-start | bytes 1032200 | tf_op jit(solution)/shard_map/ppermute | solution.py:265
  92.8 0.0 all-to-all-done
  92.8 13.8 %update_cells.2.refs_2_ = f32[640,128]{1,0:T(8,128)S(1)} custom-call(s32[3]{0:T(128)S(1)} %pad_add_fusion.refs_0_, f32[4,8]{1,0:T(4,128)S(1)} %copy-done.3, f32[640,128]{1,0:T(8,128)S(1)} %bitcast.18, f32[8,128]{1,0:T(8,128)S(1)} %slice_bitcast_fusion.refs_3_, f32[672,128]{1,0:T(8,128)S(1)} %get-tuple-element.11.refs_4_, ...), custom_call_target="tpu_custom_call" | custom-call | flops 6000000000 | bytes 2000000 | tf_op jit(solution)/shard_map/update_cells/pallas_call | solution.py:210
  106.6 0.0 collective-permute-done.3.refs_6_
  106.6 0.0 collective-permute-done.2.refs_5_
  106.7 13.8 %update_cells.3 = f32[640,128]{1,0:T(8,128)S(1)} custom-call(s32[3]{0:T(128)S(1)} %pad_add_fusion.refs_0_, f32[4,8]{1,0:T(4,128)S(1)} %copy-done.3, f32[640,128]{1,0:T(8,128)S(1)} %update_cells.2.refs_2_, f32[8,128]{1,0:T(8,128)S(1)} %slice_bitcast_fusion.refs_3_, f32[672,128]{1,0:T(8,128)S(1)} %pad_maximum_fusion.refs_4_, ...), custom_call_target="tpu_custom_call" | custom-call | flops 6000000000 | bytes 2000000 | tf_op jit(solution)/shard_map/update_cells/pallas_call | solution.py:210
  120.5 31.5 %all_to_all.10 = f32[16,40,128]{2,1,0:T(8,128)S(1)} all-to-all(f32[16,40,128]{2,1,0:T(8,128)S(1)} %bitcast.19), channel_id=1, replica_groups=mesh['member'=16,'space'=32] {'member'}, dimensions={0} | all-to-all | bytes 655360 | tf_op jit(solution)/shard_map/all_to_all | solution.py:269
  152.0 0.9 unsend.1
  (17 shorter events, 0.2 us)
Async XLA Ops:
  0.0 1.0 copy-start
  1.0 0.7 copy-start.1
  3.4 15.2 %copy-start.2 = (s32[2,1024]{1,0:T(2,128)S(1)}, s32[2,1024]{1,0:T(2,128)}, u32[]{:S(2)}) copy-start(s32[2,1024]{1,0:T(2,128)} %gp_ref.1) | copy-start | bytes 24580
  3.4 89.4 %all-to-all-start = ((f32[16,40,128]{2,1,0:T(8,128)}), f32[16,40,128]{2,1,0:T(8,128)S(1)}, u32[]{:S(2)}, u32[]{:S(2)}) async-start(f32[16,40,128]{2,1,0:T(8,128)} %bitcast.3), calls=%async_computation | async-start | bytes 655360 | tf_op jit(solution)/shard_map/all_to_all | solution.py:258
  18.6 0.7 copy-start.4
  19.3 43.1 %copy-start.5 = (f32[2,1024]{1,0:T(2,128)S(1)}, f32[2,1024]{1,0:T(2,128)}, u32[]{:S(2)}) copy-start(f32[2,1024]{1,0:T(2,128)} %param.8) | copy-start | bytes 24580
  19.3 43.1 %copy-start.6 = (f32[2,1024]{1,0:T(2,128)S(1)}, f32[2,1024]{1,0:T(2,128)}, u32[]{:S(2)}) copy-start(f32[2,1024]{1,0:T(2,128)} %param.7) | copy-start | bytes 24580
  62.6 8.6 %collective-permute-start.1 = (f32[672,128]{1,0:T(8,128)S(1)}, f32[672,128]{1,0:T(8,128)S(1)}, u32[]{:S(2)}, u32[]{:S(2)}) collective-permute-start(f32[672,128]{1,0:T(8,128)S(1)} %get-tuple-element.11.refs_4_), channel_id=1, source_target_pairs={{0,31},{1,2},{2,1},{3,4},{4,3},{5,6},{6,5},{7,8},{8,7},{9,10},{10,... | collective-permute-start | bytes 1032200 | tf_op jit(solution)/shard_map/ppermute | solution.py:261
  64.5 6.6 %collective-permute-start = (f32[672,128]{1,0:T(8,128)S(1)}, f32[672,128]{1,0:T(8,128)S(1)}, u32[]{:S(2)}, u32[]{:S(2)}) collective-permute-start(f32[672,128]{1,0:T(8,128)S(1)} %get-tuple-element.11.refs_4_), channel_id=1, source_target_pairs={{0,1},{1,0},{2,3},{3,2},{4,5},{5,4},{6,7},{7,6},{8,9},{9,8},{10,11... | collective-permute-start | bytes 1032200 | tf_op jit(solution)/shard_map/ppermute | solution.py:260
  67.8 3.3 %copy-start.3 = (f32[4,8]{1,0:T(4,128)S(1)}, f32[4,8]{1,0:T(4,128)}, u32[]{:S(2)}) copy-start(f32[4,8]{1,0:T(4,128)} %refs_1_.5) | copy-start | bytes 388
  85.6 21.0 %collective-permute-start.3 = (f32[672,128]{1,0:T(8,128)S(1)}, f32[672,128]{1,0:T(8,128)S(1)}, u32[]{:S(2)}, u32[]{:S(2)}) collective-permute-start(f32[672,128]{1,0:T(8,128)S(1)} %pad_maximum_fusion.refs_4_), channel_id=1, source_target_pairs={{0,31},{1,2},{2,1},{3,4},{4,3},{5,6},{6,5},{7,8},{8,7},{9,10},{10,... | collective-permute-start | bytes 1032200 | tf_op jit(solution)/shard_map/ppermute | solution.py:266
  87.8 18.8 %collective-permute-start.2 = (f32[672,128]{1,0:T(8,128)S(1)}, f32[672,128]{1,0:T(8,128)S(1)}, u32[]{:S(2)}, u32[]{:S(2)}) collective-permute-start(f32[672,128]{1,0:T(8,128)S(1)} %pad_maximum_fusion.refs_4_), channel_id=1, source_target_pairs={{0,1},{1,0},{2,3},{3,2},{4,5},{5,4},{6,7},{7,6},{8,9},{9,8},{10,11... | collective-permute-start | bytes 1032200 | tf_op jit(solution)/shard_map/ppermute | solution.py:265
where the time goes:
time: 154 us; the launch traced here: 153 us
  blocking collectives  74.7 us (49%)
  Pallas kernels  44.6 us (29%)
  starting transfers between devices  27.5 us (18%)
  waiting for transfers between devices  3.31 us (2%)
  local copies, waits for them, and re-layouts  2.49 us (2%)
    all_gather x1, blocking collectives, per_device(): gathered = lax.all_gather(picks, 'member', axis=0).reshape(2 * ROWS, 128)  43.1 us
    pallas_call x3, Pallas kernels, update(): pl.pallas_call(kernel, out_shape=jax.ShapeDtypeStruct((ROWS, 128), f32),...  42 us
    all_to_all x1, blocking collectives, per_device(): lax.all_to_all(cells.reshape(16, 5, 8, 128).reshape(ROWS, 128).reshape(16...  31.5 us
    all_to_all x1, starting transfers between devices, per_device(): lax.all_to_all(send.reshape(16, 40, 128), 'member', 0, 0, tiled=True)  15.2 us
    ppermute x1, starting transfers between devices, per_device(): side2 = lax.ppermute(own2, 'space', swap)  4.98 us
    ppermute x1, waiting for transfers between devices, per_device(): off = lax.ppermute(own, 'space', hop)  3.3 us
    ppermute x1, starting transfers between devices, per_device(): side = lax.ppermute(own, 'space', swap)  3.17 us
  transfers between devices with their start and end apart: 5, of which 1 were waited for; matrix products, arithmetic and copies ran while one was open for 0% of the time, Pallas kernels for 18%

commit v1 on v0

v1 whole, which is shorter than its diff:
```python
import jax
import jax.numpy as jnp
from jax import lax
from jax.experimental import pallas as pl
from jax.experimental.pallas import tpu as pltpu
from jax.sharding import PartitionSpec as P

MEMBERS = 80
CELLS = 1024
BLOCK = 16384
BIN_BITS = 11
BINS = 8
CLASSES = 4
ROWS = 640
BUNDLE = 672
MERGED = 3072
f32 = jnp.float32
bf16 = jnp.bfloat16
VM = pl.BlockSpec(memory_space=pltpu.VMEM)
SM = pl.BlockSpec(memory_space=pltpu.SMEM)
PARAMS = pltpu.CompilerParams(vmem_limit_bytes=48 * 1024 * 1024)


def split(value):
    high = value.astype(bf16)
    low = (value - high.astype(f32)).astype(bf16)
    return high, low


def pick_kernel(
    x_hbm, value_hbm, error_hbm, gp_hbm, sort_hbm, send_ref, picks_ref, par_ref,
    x_ref, value_ref, error_ref, gp_ref, sort_ref, parts_ref, sems
):
    whole = ((x_hbm, x_ref), (gp_hbm, gp_ref), (value_hbm, value_ref), (error_hbm, error_ref), (sort_hbm, sort_ref))
    copies = [pltpu.make_async_copy(src, dst, sems.at[i]) for i, (src, dst) in enumerate(whole)]
    for copy in copies:
        copy.start()
    for copy in copies:
        copy.wait()
    for c in range(128):
        d, r = c // 8, c % 8
        slab = x_ref[:, c * 128 : (c + 1) * 128]
        send_ref[pl.ds(d * 40 + r, 5, stride=8), :] = slab
    for b in range(2):
        for at, ref in enumerate((value_ref, error_ref, gp_ref, sort_ref)):
            for r in range(8):
                row = ref[b : b + 1, r * 128 : (r + 1) * 128].astype(f32)
                par_ref[b * 32 + at * 8 + r : b * 32 + at * 8 + r + 1, :] = row
    lane = lax.broadcasted_iota(jnp.int32, (128, 128), 0)
    for m in range(5):
        slabs = jnp.concatenate([send_ref[d * 40 + m * 8 : d * 40 + m * 8 + 8, :] for d in range(16)], axis=0)
        high, low = split(slabs)
        parts_ref[m * 128 : (m + 1) * 128, :128] = high
        parts_ref[m * 128 : (m + 1) * 128, 128:] = low
    for b in range(2):
        for r in range(8):
            cell = gp_ref[b : b + 1, r * 128 : (r + 1) * 128]
            onehot = jnp.where((cell & 127) == lane, 1.0, 0.0).astype(bf16)
            found = jnp.dot(
                parts_ref[...], jnp.concatenate([onehot, onehot], axis=0), preferred_element_type=f32
            )
            here = lane == (cell >> 7)
            for m in range(5):
                value = jnp.where(here, found[m * 128 : (m + 1) * 128, :], 0.0)
                picks_ref[b * 40 + m * 8 + r : b * 40 + m * 8 + r + 1, :] = jnp.sum(value, axis=0, keepdims=True)


def pick(samples, quantity, variance, grid_point, sort):
    return pl.pallas_call(
        pick_kernel,
        out_shape=(
            jax.ShapeDtypeStruct((ROWS, 128), f32),
            jax.ShapeDtypeStruct((80, 128), f32),
            jax.ShapeDtypeStruct((64, 128), f32),
        ),
        in_specs=[pl.BlockSpec(memory_space=pltpu.HBM)] * 5,
        out_specs=(VM, VM, VM),
        scratch_shapes=[
            pltpu.VMEM(samples.shape, f32),
            pltpu.VMEM(quantity.shape, f32),
            pltpu.VMEM(variance.shape, f32),
            pltpu.VMEM(grid_point.shape, jnp.int32),
            pltpu.VMEM(sort.shape, jnp.int32),
            pltpu.VMEM((640, 256), bf16),
            pltpu.SemaphoreType.DMA((5,)),
        ],
        compiler_params=pltpu.CompilerParams(vmem_limit_bytes=63 * 1024 * 1024 + 512 * 1024),
        name="pick",
    )(samples, quantity, variance, grid_point, sort)


def bundle_kernel(gathered_ref, par_ref, bundle_ref, cells_ref):
    for k in range(16):
        bundle_ref[k * 40 : (k + 1) * 40, :] = gathered_ref[k * 80 : k * 80 + 40, :]
        cells_ref[k * 40 : (k + 1) * 40, :] = gathered_ref[k * 80 + 40 : k * 80 + 80, :]
    bundle_ref[ROWS:BUNDLE, :] = par_ref[...]


def make_bundle(gathered, par):
    return pl.pallas_call(
        bundle_kernel,
        out_shape=(jax.ShapeDtypeStruct((BUNDLE, 128), f32), jax.ShapeDtypeStruct((ROWS, 128), f32)),
        in_specs=[VM, VM],
        out_specs=(VM, VM),
        compiler_params=PARAMS,
        name="bundle",
    )(gathered, par)


def taper_of(classes, tab_ref):
    rows = []
    for b in range(BINS):
        row = jnp.zeros(classes.shape, f32)
        for c in range(CLASSES):
            row = jnp.where(classes == c, tab_ref[c, b], row)
        rows.append(row)
    return rows


def prepare_cells(x_ref, e3_ref):
    for r in range(8):
        cells = x_ref[pl.ds(r, MEMBERS, stride=8), :]
        dev = cells - jnp.sum(cells, axis=0, keepdims=True) / MEMBERS
        high = dev.astype(bf16).astype(f32)
        low = dev - high
        stacked = jnp.concatenate([high, low, high, jnp.zeros((16, 128), f32)], axis=0)
        e3_ref[r * 128 : (r + 1) * 128, :] = stacked.T.astype(bf16)


def prepare_section(sec, ref, tab_ref, d3_ref, a2_ref, rows_ref, start=None, shifted=None, place_ref=None):
    width = d3_ref.shape[2] // 128
    place = ref[656:664, :].astype(jnp.int32)
    classes = ref[664:672, :].astype(jnp.int32)
    taper = taper_of(classes, tab_ref)
    if shifted is None:
        first = start - place
        rising = first >= 0
        dist = jnp.abs(first)
        bin0 = dist >> BIN_BITS
        inner = dist & ((1 << BIN_BITS) - 1)
        turn = jnp.where(rising, (1 << BIN_BITS) - inner, inner + 1)
        bin1 = jnp.where(rising, bin0 + 1, jnp.maximum(bin0 - 1, 0))
        before = jnp.zeros(classes.shape, f32)
        after = jnp.zeros(classes.shape, f32)
        for b in range(BINS):
            before = jnp.where(bin0 == b, taper[b], before)
            after = jnp.where(bin1 == b, taper[b], after)
    else:
        shifted = shifted(place)
    for r in range(8):
        tile, col = (sec * 8 + r) // width, ((sec * 8 + r) % width) * 128
        cols = slice(col, col + 128)
        prior = ref[pl.ds(r, MEMBERS, stride=8), :]
        mean = jnp.sum(prior, axis=0, keepdims=True) / MEMBERS
        dev = prior - mean
        spread = jnp.sum(dev * dev, axis=0, keepdims=True) / (MEMBERS - 1)
        value = ref[640 + r : 641 + r, :]
        error = ref[648 + r : 649 + r, :]
        total = spread + error
        scale = 1.0 / (total * (MEMBERS - 1))
        shrink = 1.0 / (1.0 + jnp.sqrt(error / total))
        step = (value - mean) - shrink * dev
        high, low = split(dev)
        d3_ref[tile, 0:80, cols] = high
        d3_ref[tile, 80:160, cols] = high
        d3_ref[tile, 160:240, cols] = low
        d3_ref[tile, 240:256, cols] = jnp.zeros((16, 128), bf16)
        high, low = split(step)
        pad = jnp.zeros((48, 128), bf16)
        a2_ref[tile, 0:80, cols] = high
        a2_ref[tile, 80:128, cols] = pad
        a2_ref[tile, 128:208, cols] = low
        a2_ref[tile, 208:256, cols] = pad
        full = (8, 128)
        if shifted is None:
            rows_ref[tile, 0:8, cols] = jnp.broadcast_to(turn[r : r + 1, :].astype(f32), full)
            rows_ref[tile, 8:16, cols] = jnp.broadcast_to(before[r : r + 1, :] * scale, full)
            rows_ref[tile, 16:24, cols] = jnp.broadcast_to(after[r : r + 1, :] * scale, full)
        else:
            place_ref[tile, :, cols] = jnp.broadcast_to(shifted[r : r + 1, :], full)
            rows_ref[tile, :, cols] = jnp.concatenate([taper[b][r : r + 1, :] * scale for b in range(BINS)], axis=0)


def add_gains(rows, weight, cov, a2_ref, tile, acc_ref):
    gain = (weight * cov).reshape(cov.shape[0] * 8, cov.shape[2])
    high, low = split(gain)
    nt = (((1,), (1,)), ((), ()))
    acc_ref[rows, :] += lax.dot_general(high, a2_ref[tile], nt, preferred_element_type=f32)
    acc_ref[rows, :128] += lax.dot_general(low, a2_ref[tile, 0:128, :], nt, preferred_element_type=f32)


def scattered(tile, dist_of, masked, e3_ref, posb_ref, d3_ref, a2_ref, rows_ref, place_ref, acc_ref):
    part = 256
    width = d3_ref.shape[2]
    for ic in range(CELLS // part):
        rows = slice(ic * part, (ic + 1) * part)
        cov = jnp.dot(e3_ref[rows, :], d3_ref[tile], preferred_element_type=f32).reshape(part // 8, 8, width)
        groups = []
        for h in range(width // 128):
            cols = slice(h * 128, (h + 1) * 128)
            place = place_ref[tile, :, cols]
            table = rows_ref[tile, :, cols]
            slabs = []
            for g in range(part // 8):
                at = ic * part + g * 8
                level = dist_of(posb_ref[at : at + 8, :], place) >> BIN_BITS
                if masked:
                    got = jnp.take_along_axis(table, level & (BINS - 1), axis=0, mode="promise_in_bounds")
                    got = jnp.where(level < BINS, got, 0.0)
                else:
                    got = jnp.take_along_axis(table, level, axis=0, mode="promise_in_bounds")
                slabs.append(got[None])
            groups.append(jnp.concatenate(slabs, axis=0))
        add_gains(rows, jnp.concatenate(groups, axis=2), cov, a2_ref, tile, acc_ref)


def place_cells(pos_ref, posb_ref, sign):
    for r in range(8):
        row = jnp.broadcast_to(pos_ref[r : r + 1, :], (128, 128))
        posb_ref[r * 128 : (r + 1) * 128, :] = row.T.astype(jnp.int32) * sign


def replay_chip_kernel(
    at_ref, tab_ref, x_ref, pos_ref, own_ref, side_ref, out_ref,
    e3_ref, posb_ref, acc_ref, d3_ref, a2_ref, rows_ref, place_ref
):
    sign = at_ref[1]
    prepare_cells(x_ref, e3_ref)
    place_cells(pos_ref, posb_ref, sign)
    work = (e3_ref, posb_ref, d3_ref, a2_ref, rows_ref, place_ref, acc_ref)
    prepare_section(
        0, own_ref, tab_ref, d3_ref, a2_ref, rows_ref, shifted=lambda place: place * sign, place_ref=place_ref
    )
    prepare_section(
        1, side_ref.at[at_ref[2]], tab_ref, d3_ref, a2_ref, rows_ref,
        shifted=lambda place: place * sign + BLOCK, place_ref=place_ref,
    )
    acc_ref[...] = jnp.zeros_like(acc_ref)
    scattered(0, lambda pos, place: jnp.abs(pos - place), False, *work)
    scattered(1, lambda pos, place: place - pos, True, *work)
    finish(x_ref, acc_ref, out_ref)


def replay_off_kernel(
    at_ref, tab_ref, x_ref, pos_ref, part_ref, off_ref, par_ref, out_ref,
    e3_ref, posb_ref, acc_ref, d3_ref, a2_ref, rows_ref, place_ref
):
    sign = at_ref[1]
    prepare_cells(x_ref, e3_ref)
    place_cells(pos_ref, posb_ref, sign)
    work = (e3_ref, posb_ref, d3_ref, a2_ref, rows_ref, place_ref, acc_ref)
    prepare_section(
        0, off_ref, tab_ref, d3_ref, a2_ref, rows_ref,
        shifted=lambda place: place * sign - BLOCK, place_ref=place_ref,
    )
    acc_ref[...] = jnp.zeros_like(acc_ref)
    scattered(0, lambda pos, place: pos - place, True, *work)
    finish(part_ref, acc_ref, out_ref)
    out_ref[ROWS:BUNDLE, :] = par_ref[...]


def replay(kernel, sections, rows, name, at, tab, *arrays):
    return pl.pallas_call(
        kernel,
        out_shape=jax.ShapeDtypeStruct((rows, 128), f32),
        in_specs=[SM, SM] + [VM] * len(arrays),
        out_specs=VM,
        scratch_shapes=[
            pltpu.VMEM((CELLS, 256), bf16),
            pltpu.VMEM((CELLS, 128), jnp.int32),
            pltpu.VMEM((CELLS, 256), f32),
            pltpu.VMEM((sections, 256, 1024), bf16),
            pltpu.VMEM((sections, 256, 1024), bf16),
            pltpu.VMEM((sections, 8, 1024), f32),
            pltpu.VMEM((sections, 8, 1024), jnp.int32),
        ],
        compiler_params=PARAMS,
        cost_estimate=pl.CostEstimate(flops=4_000_000_000 * sections, bytes_accessed=2_000_000, transcendentals=0),
        name=name,
    )(at, tab, *arrays)


def finish(x_ref, acc_ref, out_ref):
    for r in range(8):
        rows = slice(r * 128, (r + 1) * 128)
        step = (acc_ref[rows, :128] + acc_ref[rows, 128:]).T
        out_ref[pl.ds(r, MEMBERS, stride=8), :] = x_ref[pl.ds(r, MEMBERS, stride=8), :] + step[:MEMBERS, :]


def update_kernel(at_ref, tab_ref, x_ref, own_ref, side_ref, off_ref, out_ref, e3_ref, d3_ref, a2_ref, rows_ref, acc_ref):
    start, sign = at_ref[0], at_ref[1]
    prepare_cells(x_ref, e3_ref)
    sections = ((own_ref, start), (side_ref.at[at_ref[2]], start - sign * BLOCK), (off_ref, start + sign * BLOCK))
    for sec, (ref, first) in enumerate(sections):
        prepare_section(sec, ref, tab_ref, d3_ref, a2_ref, rows_ref, start=first)
    acc_ref[...] = jnp.zeros_like(acc_ref)
    tiles, _, width = d3_ref.shape
    part = CELLS

    def tile_step(tile, carry):
        for ic in range(CELLS // part):
            rows = slice(ic * part, (ic + 1) * part)
            shape = (part // 8, 8, width)
            cov = jnp.dot(e3_ref[rows, :], d3_ref[tile], preferred_element_type=f32).reshape(shape)
            at = lax.broadcasted_iota(jnp.int32, (part, width), 0).astype(f32).reshape(shape) + float(ic * part)
            turn = rows_ref[tile, 0:8, :][None]
            weight = jnp.where(at >= turn, rows_ref[tile, 16:24, :][None], rows_ref[tile, 8:16, :][None])
            add_gains(rows, weight, cov, a2_ref, tile, acc_ref)
        return carry

    lax.fori_loop(0, tiles, tile_step, 0, unroll=2)
    finish(x_ref, acc_ref, out_ref)


def update(at, tab, x, own, side, off):
    width = 512
    tiles = MERGED // width
    return pl.pallas_call(
        update_kernel,
        out_shape=jax.ShapeDtypeStruct((ROWS, 128), f32),
        in_specs=[SM, SM, VM, VM, VM, VM],
        out_specs=VM,
        scratch_shapes=[
            pltpu.VMEM((CELLS, 256), bf16),
            pltpu.VMEM((tiles, 256, width), bf16),
            pltpu.VMEM((tiles, 256, width), bf16),
            pltpu.VMEM((tiles, 24, width), f32),
            pltpu.VMEM((CELLS, 256), f32),
        ],
        compiler_params=PARAMS,
        cost_estimate=pl.CostEstimate(flops=9_000_000_000, bytes_accessed=2_000_000, transcendentals=0),
        name="update_cells",
    )(at, tab, x, own, side, off)


def unsend_kernel(x_ref, out_ref):
    for c in range(128):
        d, r = c // 8, c % 8
        out_ref[:, c * 128 : (c + 1) * 128] = x_ref[pl.ds(d * 40 + r, 5, stride=8), :]


def unsend(x):
    return pl.pallas_call(
        unsend_kernel,
        out_shape=jax.ShapeDtypeStruct((5, BLOCK), f32),
        in_specs=[VM],
        out_specs=VM,
        compiler_params=PARAMS,
        name="unsend",
    )(x)


def per_device(samples, quantity, variance, grid_point, sort, tab):
    count = lax.axis_size("space")
    space = lax.axis_index("space")
    member = lax.axis_index("member")
    pairs = [[i, i + 1] for i in range(0, count, 2)]
    hop = [(i, (i + (1 if i % 2 else -1)) % count) for i in range(count)]
    odd = space % 2
    at = jnp.stack([member * CELLS, 1 - 2 * odd, 1 - odd]).astype(jnp.int32)

    send, picks, par = pick(samples, quantity, variance, grid_point, sort)
    par = par.reshape(2, 32, 128)
    gathered = lax.all_gather(picks, "member", axis=0).reshape(2 * ROWS, 128)
    own, second = make_bundle(gathered, par[0])
    send, own = lax.optimization_barrier((send, own))
    cells = lax.all_to_all(send.reshape(16, 40, 128), "member", 0, 0, tiled=True).reshape(ROWS, 128)
    off = lax.ppermute(own, "space", hop)
    side = lax.all_gather(own, "space", axis_index_groups=pairs)
    pos = par[1, 16:24]
    part = replay(replay_chip_kernel, 2, ROWS, "replay_chip", at, tab, second, pos, own, side)
    own2 = replay(replay_off_kernel, 1, BUNDLE, "replay_off", at, tab, second, pos, part, off, par[1])
    off2 = lax.ppermute(own2, "space", hop)
    side2 = lax.all_gather(own2, "space", axis_index_groups=pairs)
    cells = update(at, tab, cells, own, side, off)
    cells = update(at, tab, cells, own2, side2, off2)
    back = lax.all_to_all(cells.reshape(16, 40, 128), "member", 0, 0, tiled=True)
    return unsend(back.reshape(ROWS, 128))


def solution(mesh):
    in_specs = (
        P("member", "space"),
        P(None, "space"),
        P(None, "space"),
        P(None, "space"),
        P(None, "space"),
        P(),
    )
    return jax.shard_map(
        per_device, mesh=mesh, in_specs=in_specs, out_specs=P("member", "space"), check_vma=False
    )
```

time: 154 us -> 124 us (0.81)
  starting transfers between devices: 27.5 us -> 10.9 us
  Pallas kernels: 44.6 us -> 29.4 us
  blocking collectives: 74.7 us -> 79 us
  waiting for transfers between devices: 3.31 us -> 0.01 us
    pallas_call x3 -> x4, Pallas kernels: 42 us -> 25.1 us  [the longest x2 15.2 us: update(): pl.pallas_call(update_kernel, out_shape=jax.ShapeDtypeStruct((ROWS, 128),...]
    all_to_all x1, starting transfers between devices: 15.2 us -> 6.13 us  [per_device(): lax.all_to_all(send.reshape(16, 40, 128), 'member', 0, 0, tiled=True)]
    ppermute x2 -> x0, starting transfers between devices: 8.15 us -> none  [the longest x1 4.98 us: per_device(): side2 = lax.ppermute(own2, 'space', swap)]
    all_gather x0 -> x2, blocking collectives: none -> 5.94 us  [the longest x1 3.09 us: per_device(): side = lax.all_gather(own, 'space', axis_index_groups=pairs)]
    all_gather x1, blocking collectives: 43.1 us -> 39.6 us  [per_device(): gathered = lax.all_gather(picks, 'member', axis=0).reshape(2 * ROWS, 128)]
    ppermute x1, waiting for transfers between devices: 3.3 us -> 0.01 us  [per_device(): off = lax.ppermute(own, 'space', hop)]
    all_to_all x1, blocking collectives: 31.5 us -> 33.4 us  [per_device(): lax.all_to_all(cells.reshape(16, 40, 128), 'member', 0, 0, tiled=True)]
    unnamed x14 -> x4, local copies, waits for them, and re-layouts: 2.43 us -> 0.71 us
  transfers between devices with their start and end apart: 5 -> 3, of which waited for: 1 -> 0; matrix products, arithmetic and copies ran while one was open for 0% -> 1% of each run, Pallas kernels for 18% -> 14%
where the time goes in v1:
time: 124 us; the launch traced here: 122 us
  blocking collectives  79 us (64%)
  Pallas kernels  29.4 us (24%)
  starting transfers between devices  10.9 us (9%)
  local copies, waits for them, and re-layouts  2.13 us (2%)
    all_gather x1, blocking collectives, per_device(): gathered = lax.all_gather(picks, 'member', axis=0).reshape(2 * ROWS, 128)  39.6 us
    all_to_all x1, blocking collectives, per_device(): lax.all_to_all(cells.reshape(16, 40, 128), 'member', 0, 0, tiled=True)  33.4 us
    pallas_call x2, Pallas kernels, update(): pl.pallas_call(update_kernel, out_shape=jax.ShapeDtypeStruct((ROWS, 128),...  15.2 us
    pallas_call x2, Pallas kernels, replay(): pl.pallas_call(kernel, out_shape=jax.ShapeDtypeStruct((rows, 128), f32),...  9.93 us
    all_to_all x1, starting transfers between devices, per_device(): lax.all_to_all(send.reshape(16, 40, 128), 'member', 0, 0, tiled=True)  6.13 us
    pallas_call x1, Pallas kernels, pick(): pl.pallas_call(pick_kernel, out_shape=(jax.ShapeDtypeStruct((ROWS, 128),...  3.35 us
    all_gather x1, blocking collectives, per_device(): side = lax.all_gather(own, 'space', axis_index_groups=pairs)  3.09 us
    all_gather x1, blocking collectives, per_device(): side2 = lax.all_gather(own2, 'space', axis_index_groups=pairs)  2.85 us
  transfers between devices with their start and end apart: 3, of which 0 were waited for; matrix products, arithmetic and copies ran while one was open for 1% of the time, Pallas kernels for 14%

profile of v1, /device:TPU:24, one launch (start us, length us, event | category | flops | bytes accessed | tf_op | source)
XLA Modules:
  0.0 121.6 jit_solution(18178797923676207840)
XLA Ops:
  0.0 3.4 %pick.1 = (f32[640,128]{1,0:T(8,128)}, f32[80,128]{1,0:T(8,128)}, f32[64,128]{1,0:T(8,128)}) custom-call(f32[5,16384]{1,0:T(8,128)} %x_hbm.1, f32[2,1024]{1,0:T(2,128)} %value_hbm.1, f32[2,1024]{1,0:T(2,128)} %error_hbm.1, s32[2,1024]{1,0:T(2,128)} %gp_hbm.1, s32[2,1024]{1,0:T(2,128)} %sort_hbm.1), custom_call_target="tpu_custom_call" | custom-call | tf_op jit(solution)/shard_map/pick/pallas_call | solution.py:69
  3.4 0.0 copy-start.1
  3.4 0.7 fusion
  4.1 0.0 copy-done.1
  4.1 39.6 %all-gather.gathered_ref = f32[1280,128]{1,0:T(8,128)S(1)} all-gather(f32[80,128]{1,0:T(8,128)S(1)} %copy-done.1), channel_id=2, replica_groups=mesh['member'=16,'space'=32] {'member'}, dimensions={0}, use_global_device_ids=true | all-gather | bytes 696320 | tf_op jit(solution)/shard_map/all_gather | solution.py:364
  43.8 6.1 %all-to-all-start = ((f32[16,40,128]{2,1,0:T(8,128)}), f32[16,40,128]{2,1,0:T(8,128)S(1)}, u32[]{:S(2)}, u32[]{:S(2)}) async-start(f32[16,40,128]{2,1,0:T(8,128)} %bitcast.3), calls=%async_computation | async-start | bytes 655360 | tf_op jit(solution)/shard_map/all_to_all | solution.py:367
  49.9 1.9 %collective-permute-start = (f32[672,128]{1,0:T(8,128)S(1)}, f32[672,128]{1,0:T(8,128)S(1)}, u32[]{:S(2)}, u32[]{:S(2)}) collective-permute-start(f32[672,128]{1,0:T(8,128)S(1)} %get-tuple-element.17.own_ref), channel_id=1, source_target_pairs={{0,31},{1,2},{2,1},{3,4},{4,3},{5,6},{6,5},{7,8},{8,7},{9,10},{10,... | collective-permute-start | bytes 1032200 | tf_op jit(solution)/shard_map/ppermute | solution.py:368
  51.9 3.1 %all-gather.1 = f32[1344,128]{1,0:T(8,128)S(1)} all-gather(f32[672,128]{1,0:T(8,128)S(1)} %get-tuple-element.17.own_ref), channel_id=3, replica_groups={{0,1},{2,3},{4,5},{6,7},{8,9},{10,11},{12,13},{14,15},{16,17},{18,19},{..., dimensions={0}, use_global_device_ids=true | all-gather | bytes 1032192 | tf_op jit(solution)/shard_map/all_gather | solution.py:369
  54.9 0.7 slice_bitcast_fusion.pos_ref
  55.6 0.1 pad_add_fusion.at_ref
  55.7 0.0 copy-start
  55.7 0.7 copy-done
  56.4 6.2 %replay_chip.1.part_ref = f32[640,128]{1,0:T(8,128)S(1)} custom-call(s32[3]{0:T(128)S(1)} %pad_add_fusion.at_ref, f32[4,8]{1,0:T(4,128)S(1)} %copy-done, f32[640,128]{1,0:T(8,128)S(1)} %get-tuple-element.18.x_ref, f32[8,128]{1,0:T(8,128)S(1)} %slice_bitcast_fusion.pos_ref, f32[672,128]{1,0:T(8,128)S(1)} %get-tuple-element.17.own_ref, f32[2,672,128]{2,1,0:T(8,128)S(1)} %bitcast.13), custom_call_target="tpu_custom_call" | custom-call | flops 8000000000 | bytes 2000000 | tf_op jit(solution)/shard_map/replay_chip/pallas_call | solution.py:263
  62.6 0.0 collective-permute-done.off_ref
  62.6 3.7 %replay_off.1.own_ref = f32[672,128]{1,0:T(8,128)S(1)} custom-call(s32[3]{0:T(128)S(1)} %pad_add_fusion.at_ref, f32[4,8]{1,0:T(4,128)S(1)} %copy-done, f32[640,128]{1,0:T(8,128)S(1)} %get-tuple-element.18.x_ref, f32[8,128]{1,0:T(8,128)S(1)} %slice_bitcast_fusion.pos_ref, f32[640,128]{1,0:T(8,128)S(1)} %replay_chip.1.part_ref, ...), custom_call_target="tpu_custom_call" | custom-call | flops 4000000000 | bytes 2000000 | tf_op jit(solution)/shard_map/replay_off/pallas_call | solution.py:263
  66.3 2.9 %collective-permute-start.1 = (f32[672,128]{1,0:T(8,128)S(1)}, f32[672,128]{1,0:T(8,128)S(1)}, u32[]{:S(2)}, u32[]{:S(2)}) collective-permute-start(f32[672,128]{1,0:T(8,128)S(1)} %replay_off.1.own_ref), channel_id=1, source_target_pairs={{0,31},{1,2},{2,1},{3,4},{4,3},{5,6},{6,5},{7,8},{8,7},{9,10},{10,... | collective-permute-start | bytes 1032200 | tf_op jit(solution)/shard_map/ppermute | solution.py:373
  69.2 2.9 %all-gather.2 = f32[1344,128]{1,0:T(8,128)S(1)} all-gather(f32[672,128]{1,0:T(8,128)S(1)} %replay_off.1.own_ref), channel_id=4, replica_groups={{0,1},{2,3},{4,5},{6,7},{8,9},{10,11},{12,13},{14,15},{16,17},{18,19},{..., dimensions={0}, use_global_device_ids=true | all-gather | bytes 1032192 | tf_op jit(solution)/shard_map/all_gather | solution.py:374
  72.0 0.0 all-to-all-done
  72.0 7.6 %update_cells.2.x_ref = f32[640,128]{1,0:T(8,128)S(1)} custom-call(s32[3]{0:T(128)S(1)} %pad_add_fusion.at_ref, f32[4,8]{1,0:T(4,128)S(1)} %copy-done, f32[640,128]{1,0:T(8,128)S(1)} %bitcast.16, f32[672,128]{1,0:T(8,128)S(1)} %get-tuple-element.17.own_ref, f32[2,672,128]{2,1,0:T(8,128)S(1)} %bitcast.14, f32[672,128]{1,0:T(8,128)S(1)} %collective-permute-done.off_ref), custom_call_target="tpu_custom_call" | custom-call | flops 8999999488 | bytes 2000000 | tf_op jit(solution)/shard_map/update_cells/pallas_call | solution.py:318
  79.6 0.0 collective-permute-done.1.off_ref
  79.7 7.6 %update_cells.3 = f32[640,128]{1,0:T(8,128)S(1)} custom-call(s32[3]{0:T(128)S(1)} %pad_add_fusion.at_ref, f32[4,8]{1,0:T(4,128)S(1)} %copy-done, f32[640,128]{1,0:T(8,128)S(1)} %update_cells.2.x_ref, f32[672,128]{1,0:T(8,128)S(1)} %replay_off.1.own_ref, f32[2,672,128]{2,1,0:T(8,128)S(1)} %bitcast.15, f32[672,128]{1,0:T(8,128)S(1)} %collective-permute-done.1.off_ref), custom_call_target="tpu_custom_call" | custom-call | flops 8999999488 | bytes 2000000 | tf_op jit(solution)/shard_map/update_cells/pallas_call | solution.py:318
  87.3 33.4 %all_to_all.10 = f32[16,40,128]{2,1,0:T(8,128)S(1)} all-to-all(f32[16,40,128]{2,1,0:T(8,128)S(1)} %bitcast.17), channel_id=1, replica_groups=mesh['member'=16,'space'=32] {'member'}, dimensions={0} | all-to-all | bytes 655360 | tf_op jit(solution)/shard_map/all_to_all | solution.py:377
  120.7 0.9 unsend.1
  (1 shorter events, 0.0 us)
Async XLA Ops:
  3.4 0.8 copy-start.1
  43.8 28.3 %all-to-all-start = ((f32[16,40,128]{2,1,0:T(8,128)}), f32[16,40,128]{2,1,0:T(8,128)S(1)}, u32[]{:S(2)}, u32[]{:S(2)}) async-start(f32[16,40,128]{2,1,0:T(8,128)} %bitcast.3), calls=%async_computation | async-start | bytes 655360 | tf_op jit(solution)/shard_map/all_to_all | solution.py:367
  49.9 12.7 %collective-permute-start = (f32[672,128]{1,0:T(8,128)S(1)}, f32[672,128]{1,0:T(8,128)S(1)}, u32[]{:S(2)}, u32[]{:S(2)}) collective-permute-start(f32[672,128]{1,0:T(8,128)S(1)} %get-tuple-element.17.own_ref), channel_id=1, source_target_pairs={{0,31},{1,2},{2,1},{3,4},{4,3},{5,6},{6,5},{7,8},{8,7},{9,10},{10,... | collective-permute-start | bytes 1032200 | tf_op jit(solution)/shard_map/ppermute | solution.py:368
  55.7 0.7 copy-start
  66.3 13.3 %collective-permute-start.1 = (f32[672,128]{1,0:T(8,128)S(1)}, f32[672,128]{1,0:T(8,128)S(1)}, u32[]{:S(2)}, u32[]{:S(2)}) collective-permute-start(f32[672,128]{1,0:T(8,128)S(1)} %replay_off.1.own_ref), channel_id=1, source_target_pairs={{0,31},{1,2},{2,1},{3,4},{4,3},{5,6},{6,5},{7,8},{8,7},{9,10},{10,... | collective-permute-start | bytes 1032200 | tf_op jit(solution)/shard_map/ppermute | solution.py:373

commit v2 on v1

v2 whole, which is shorter than its diff:
```python
import jax
import jax.numpy as jnp
from jax import lax
from jax.experimental import pallas as pl
from jax.experimental.pallas import tpu as pltpu
from jax.sharding import PartitionSpec as P

MEMBERS = 80
CELLS = 1024
BLOCK = 16384
BIN_BITS = 11
BINS = 8
CLASSES = 4
ROWS = 640
BUNDLE = 96
VALUE, ERROR, PLACE, KIND, TABLE = 80, 81, 82, 83, 88
MERGED = 3072
CHUNKS = 4
PICK_VMEM = 62 * 1024 * 1024 + 768 * 1024
f32 = jnp.float32
bf16 = jnp.bfloat16
VM = pl.BlockSpec(memory_space=pltpu.VMEM)
SM = pl.BlockSpec(memory_space=pltpu.SMEM)
PARAMS = pltpu.CompilerParams(vmem_limit_bytes=48 * 1024 * 1024)


def split(value):
    high = value.astype(bf16)
    low = (value - high.astype(f32)).astype(bf16)
    return high, low


def pick_kernel(
    x_hbm, value_hbm, error_hbm, gp_hbm, sort_hbm, tab_hbm, send_ref, picks_ref, par_ref,
    x_ref, value_ref, error_ref, gp_ref, sort_ref, tab_ref, parts_ref, sems
):
    small = ((value_hbm, value_ref), (error_hbm, error_ref), (gp_hbm, gp_ref), (sort_hbm, sort_ref), (tab_hbm, tab_ref))
    copies = []
    for i in range(CHUNKS):
        cols = pl.ds(i * (BLOCK // CHUNKS), BLOCK // CHUNKS)
        copies.append(pltpu.make_async_copy(x_hbm.at[:, cols], x_ref.at[:, cols], sems.at[i]))
    for i, (src, dst) in enumerate(small):
        copies.append(pltpu.make_async_copy(src, dst, sems.at[CHUNKS + i]))
    for copy in copies[CHUNKS:] + copies[:CHUNKS]:
        copy.start()
    for copy in copies[CHUNKS:]:
        copy.wait()
    for b in range(2):
        for at, ref in enumerate((value_ref, error_ref, gp_ref, sort_ref)):
            par_ref[b * 16 + at : b * 16 + at + 1, :] = ref[b : b + 1, :].astype(f32)
        par_ref[b * 16 + 4 : b * 16 + 8, :] = jnp.zeros((4, CELLS), f32)
        kind = sort_ref[b : b + 1, :]
        for level in range(BINS):
            row = jnp.zeros((1, CELLS), f32)
            for c in range(CLASSES):
                row = jnp.where(kind == c, tab_ref[c : c + 1, level : level + 1], row)
            par_ref[b * 16 + 8 + level : b * 16 + 9 + level, :] = row
    each = 16 // CHUNKS
    for i in range(CHUNKS):
        copies[i].wait()
        for c in range(i * 8 * each, (i + 1) * 8 * each):
            d, r = c // 8, c % 8
            send_ref[pl.ds(d * 40 + r, 5, stride=8), :] = x_ref[:, c * 128 : (c + 1) * 128]
        for m in range(5):
            begin = i * each * 40 + m * 8
            slabs = jnp.concatenate([send_ref[begin + d * 40 : begin + d * 40 + 8, :] for d in range(each)], axis=0)
            high, low = split(slabs)
            rows = slice(m * 128 + i * each * 8, m * 128 + (i + 1) * each * 8)
            parts_ref[rows, :128] = high
            parts_ref[rows, 128:] = low
    lane = lax.broadcasted_iota(jnp.int32, (128, 256), 0)
    for b in range(2):
        for h in range(4):
            cell = gp_ref[b : b + 1, h * 256 : (h + 1) * 256]
            onehot = jnp.where((cell & 127) == lane, 1.0, 0.0).astype(bf16)
            found = jnp.dot(
                parts_ref[...], jnp.concatenate([onehot, onehot], axis=0), preferred_element_type=f32
            )
            here = lane == (cell >> 7)
            for m in range(5):
                value = jnp.where(here, found[m * 128 : (m + 1) * 128, :], 0.0)
                value = jnp.sum(value, axis=0, keepdims=True)
                row = b * 40 + m * 8 + h * 2
                picks_ref[row : row + 1, :] = value[:, :128]
                picks_ref[row + 1 : row + 2, :] = value[:, 128:]


def pick(samples, quantity, variance, grid_point, sort, tab):
    return pl.pallas_call(
        pick_kernel,
        out_shape=(
            jax.ShapeDtypeStruct((ROWS, 128), f32),
            jax.ShapeDtypeStruct((80, 128), f32),
            jax.ShapeDtypeStruct((32, CELLS), f32),
        ),
        in_specs=[pl.BlockSpec(memory_space=pltpu.HBM)] * 6,
        out_specs=(VM, VM, VM),
        scratch_shapes=[
            pltpu.VMEM(samples.shape, f32),
            pltpu.VMEM(quantity.shape, f32),
            pltpu.VMEM(variance.shape, f32),
            pltpu.VMEM(grid_point.shape, jnp.int32),
            pltpu.VMEM(sort.shape, jnp.int32),
            pltpu.VMEM(tab.shape, f32),
            pltpu.VMEM((640, 256), bf16),
            pltpu.SemaphoreType.DMA((CHUNKS + 5,)),
        ],
        compiler_params=pltpu.CompilerParams(vmem_limit_bytes=PICK_VMEM),
        name="pick",
    )(samples, quantity, variance, grid_point, sort, tab)


def bundle_kernel(gathered_ref, par_ref, bundle_ref, cells_ref, first_ref, second_ref):
    for k in range(16):
        first_ref[k * 40 : (k + 1) * 40, :] = gathered_ref[k * 80 : k * 80 + 40, :]
        second_ref[k * 40 : (k + 1) * 40, :] = gathered_ref[k * 80 + 40 : k * 80 + 80, :]
    for r in range(8):
        cols = slice(r * 128, (r + 1) * 128)
        bundle_ref[0:MEMBERS, cols] = first_ref[pl.ds(r, MEMBERS, stride=8), :]
        cells_ref[:, cols] = second_ref[pl.ds(r, MEMBERS, stride=8), :]
    bundle_ref[MEMBERS:BUNDLE, :] = par_ref[0:16, :]


def make_bundle(gathered, par):
    return pl.pallas_call(
        bundle_kernel,
        out_shape=(jax.ShapeDtypeStruct((BUNDLE, CELLS), f32), jax.ShapeDtypeStruct((MEMBERS, CELLS), f32)),
        in_specs=[VM, VM],
        out_specs=(VM, VM),
        scratch_shapes=[pltpu.VMEM((ROWS, 128), f32), pltpu.VMEM((ROWS, 128), f32)],
        compiler_params=PARAMS,
        name="bundle",
    )(gathered, par)


def prepare_cells(x_ref, e3_ref):
    for r in range(8):
        cells = x_ref[:, r * 128 : (r + 1) * 128]
        dev = cells - jnp.sum(cells, axis=0, keepdims=True) / MEMBERS
        high = dev.astype(bf16).astype(f32)
        low = dev - high
        stacked = jnp.concatenate([high, low, high, jnp.zeros((16, 128), f32)], axis=0)
        e3_ref[r * 128 : (r + 1) * 128, :] = stacked.T.astype(bf16)


def prepare_section(sec, ref, d3_ref, a2_ref, rows_ref, start=None, shifted=None, place_ref=None):
    width = d3_ref.shape[2] // 128
    for r in range(8):
        tile, col = (sec * 8 + r) // width, ((sec * 8 + r) % width) * 128
        cols = slice(col, col + 128)
        here = slice(r * 128, (r + 1) * 128)
        prior = ref[0:MEMBERS, here]
        mean = jnp.sum(prior, axis=0, keepdims=True) / MEMBERS
        dev = prior - mean
        spread = jnp.sum(dev * dev, axis=0, keepdims=True) / (MEMBERS - 1)
        value = ref[VALUE : VALUE + 1, here]
        error = ref[ERROR : ERROR + 1, here]
        place = ref[PLACE : PLACE + 1, here].astype(jnp.int32)
        total = spread + error
        scale = 1.0 / (total * (MEMBERS - 1))
        shrink = 1.0 / (1.0 + jnp.sqrt(error / total))
        step = (value - mean) - shrink * dev
        high, low = split(dev)
        d3_ref[tile, 0:80, cols] = high
        d3_ref[tile, 80:160, cols] = high
        d3_ref[tile, 160:240, cols] = low
        d3_ref[tile, 240:256, cols] = jnp.zeros((16, 128), bf16)
        high, low = split(step)
        pad = jnp.zeros((48, 128), bf16)
        a2_ref[tile, 0:80, cols] = high
        a2_ref[tile, 80:128, cols] = pad
        a2_ref[tile, 128:208, cols] = low
        a2_ref[tile, 208:256, cols] = pad
        full = (8, 128)
        table = ref[TABLE : TABLE + BINS, here] * scale
        if shifted is None:
            first = start - place
            rising = first >= 0
            dist = jnp.abs(first)
            bin0 = dist >> BIN_BITS
            inner = dist & ((1 << BIN_BITS) - 1)
            turn = jnp.where(rising, (1 << BIN_BITS) - inner, inner + 1)
            bin1 = jnp.where(rising, bin0 + 1, jnp.maximum(bin0 - 1, 0))
            level = lax.broadcasted_iota(jnp.int32, full, 0)
            before = jnp.sum(jnp.where(level == bin0, table, 0.0), axis=0, keepdims=True)
            after = jnp.sum(jnp.where(level == bin1, table, 0.0), axis=0, keepdims=True)
            rows_ref[tile, 0:8, cols] = jnp.broadcast_to(turn.astype(f32), full)
            rows_ref[tile, 8:16, cols] = jnp.broadcast_to(before, full)
            rows_ref[tile, 16:24, cols] = jnp.broadcast_to(after, full)
        else:
            place_ref[tile, :, cols] = jnp.broadcast_to(shifted(place), full)
            rows_ref[tile, :, cols] = table


def add_gains(rows, weight, cov, a2_ref, tile, acc_ref):
    gain = (weight * cov).reshape(cov.shape[0] * 8, cov.shape[2])
    high, low = split(gain)
    nt = (((1,), (1,)), ((), ()))
    acc_ref[rows, :] += lax.dot_general(high, a2_ref[tile], nt, preferred_element_type=f32)
    acc_ref[rows, :128] += lax.dot_general(low, a2_ref[tile, 0:128, :], nt, preferred_element_type=f32)


def scattered(tile, dist_of, masked, e3_ref, posb_ref, d3_ref, a2_ref, rows_ref, place_ref, acc_ref):
    part = 256
    width = d3_ref.shape[2]
    for ic in range(CELLS // part):
        rows = slice(ic * part, (ic + 1) * part)
        cov = jnp.dot(e3_ref[rows, :], d3_ref[tile], preferred_element_type=f32).reshape(part // 8, 8, width)
        groups = []
        for h in range(width // 128):
            cols = slice(h * 128, (h + 1) * 128)
            place = place_ref[tile, :, cols]
            table = rows_ref[tile, :, cols]
            slabs = []
            for g in range(part // 8):
                at = ic * part + g * 8
                level = dist_of(posb_ref[at : at + 8, :], place) >> BIN_BITS
                if masked:
                    got = jnp.take_along_axis(table, level & (BINS - 1), axis=0, mode="promise_in_bounds")
                    got = jnp.where(level < BINS, got, 0.0)
                else:
                    got = jnp.take_along_axis(table, level, axis=0, mode="promise_in_bounds")
                slabs.append(got[None])
            groups.append(jnp.concatenate(slabs, axis=0))
        add_gains(rows, jnp.concatenate(groups, axis=2), cov, a2_ref, tile, acc_ref)


def place_cells(par_ref, posb_ref, sign):
    for r in range(8):
        row = jnp.broadcast_to(par_ref[18:19, r * 128 : (r + 1) * 128], (128, 128))
        posb_ref[r * 128 : (r + 1) * 128, :] = row.T.astype(jnp.int32) * sign


def replay_kernel(
    at_ref, par_ref, x_ref, own_ref, side_ref, off_ref, out_ref,
    e3_ref, posb_ref, acc_ref, d3_ref, a2_ref, rows_ref, place_ref
):
    sign = at_ref[1]
    prepare_cells(x_ref, e3_ref)
    place_cells(par_ref, posb_ref, sign)
    work = (e3_ref, posb_ref, d3_ref, a2_ref, rows_ref, place_ref, acc_ref)
    sections = (
        (own_ref, lambda place: place * sign),
        (side_ref.at[at_ref[2]], lambda place: place * sign + BLOCK),
        (off_ref, lambda place: place * sign - BLOCK),
    )
    for sec, (ref, shifted) in enumerate(sections):
        prepare_section(sec, ref, d3_ref, a2_ref, rows_ref, shifted=shifted, place_ref=place_ref)
    acc_ref[...] = jnp.zeros_like(acc_ref)
    scattered(0, lambda pos, place: jnp.abs(pos - place), False, *work)
    scattered(1, lambda pos, place: place - pos, True, *work)
    scattered(2, lambda pos, place: pos - place, True, *work)
    finish(x_ref, acc_ref, out_ref)
    out_ref[MEMBERS:BUNDLE, :] = par_ref[16:32, :]


def replay(kernel, sections, name, at, par, *arrays):
    return pl.pallas_call(
        kernel,
        out_shape=jax.ShapeDtypeStruct((BUNDLE, CELLS), f32),
        in_specs=[SM, VM] + [VM] * len(arrays),
        out_specs=VM,
        scratch_shapes=[
            pltpu.VMEM((CELLS, 256), bf16),
            pltpu.VMEM((CELLS, 128), jnp.int32),
            pltpu.VMEM((CELLS, 256), f32),
            pltpu.VMEM((sections, 256, 1024), bf16),
            pltpu.VMEM((sections, 256, 1024), bf16),
            pltpu.VMEM((sections, 8, 1024), f32),
            pltpu.VMEM((sections, 8, 1024), jnp.int32),
        ],
        compiler_params=PARAMS,
        cost_estimate=pl.CostEstimate(flops=4_000_000_000 * sections, bytes_accessed=2_000_000, transcendentals=0),
        name=name,
    )(at, par, *arrays)


def finish(x_ref, acc_ref, out_ref, strided=False):
    for r in range(8):
        rows = slice(r * 128, (r + 1) * 128)
        step = (acc_ref[rows, :128] + acc_ref[rows, 128:]).T
        value = x_ref[:, rows] + step[:MEMBERS, :]
        if strided:
            out_ref[pl.ds(r, MEMBERS, stride=8), :] = value
        else:
            out_ref[0:MEMBERS, rows] = value


def update_kernel(
    last, at_ref, cells_ref, own_ref, side_ref, off_ref, out_ref, x_ref, e3_ref, d3_ref, a2_ref, rows_ref, acc_ref
):
    start, sign = at_ref[0], at_ref[1]
    if last:
        x_ref = cells_ref
    else:
        for r in range(8):
            x_ref[:, r * 128 : (r + 1) * 128] = cells_ref[pl.ds(r, MEMBERS, stride=8), :]
    prepare_cells(x_ref, e3_ref)
    sections = ((own_ref, start), (side_ref.at[0 if last else at_ref[2]], start - sign * BLOCK), (off_ref, start + sign * BLOCK))
    for sec, (ref, first) in enumerate(sections):
        prepare_section(sec, ref, d3_ref, a2_ref, rows_ref, start=first)
    acc_ref[...] = jnp.zeros_like(acc_ref)
    tiles, _, width = d3_ref.shape
    part = CELLS

    def tile_step(tile, carry):
        for ic in range(CELLS // part):
            rows = slice(ic * part, (ic + 1) * part)
            shape = (part // 8, 8, width)
            cov = jnp.dot(e3_ref[rows, :], d3_ref[tile], preferred_element_type=f32).reshape(shape)
            at = lax.broadcasted_iota(jnp.int32, (part, width), 0).astype(f32).reshape(shape) + float(ic * part)
            turn = rows_ref[tile, 0:8, :][None]
            weight = jnp.where(at >= turn, rows_ref[tile, 16:24, :][None], rows_ref[tile, 8:16, :][None])
            add_gains(rows, weight, cov, a2_ref, tile, acc_ref)
        return carry

    lax.fori_loop(0, tiles, tile_step, 0, unroll=tiles)
    finish(x_ref, acc_ref, out_ref, strided=last)


def update(last, at, x, own, side, off):
    def kernel(*refs):
        update_kernel(last, *refs)

    width = 768
    tiles = MERGED // width
    return pl.pallas_call(
        kernel,
        out_shape=jax.ShapeDtypeStruct((ROWS, 128) if last else (MEMBERS, CELLS), f32),
        in_specs=[SM, VM, VM, VM, VM],
        out_specs=VM,
        scratch_shapes=[
            pltpu.VMEM((MEMBERS, CELLS), f32),
            pltpu.VMEM((CELLS, 256), bf16),
            pltpu.VMEM((tiles, 256, width), bf16),
            pltpu.VMEM((tiles, 256, width), bf16),
            pltpu.VMEM((tiles, 24, width), f32),
            pltpu.VMEM((CELLS, 256), f32),
        ],
        compiler_params=PARAMS,
        cost_estimate=pl.CostEstimate(flops=9_000_000_000, bytes_accessed=2_000_000, transcendentals=0),
        name="update_last" if last else "update_first",
    )(at, x, own, side, off)


def unsend_kernel(x_ref, out_ref):
    for c in range(128):
        d, r = c // 8, c % 8
        out_ref[:, c * 128 : (c + 1) * 128] = x_ref[pl.ds(d * 40 + r, 5, stride=8), :]


def unsend(x):
    return pl.pallas_call(
        unsend_kernel,
        out_shape=jax.ShapeDtypeStruct((5, BLOCK), f32),
        in_specs=[VM],
        out_specs=VM,
        compiler_params=PARAMS,
        name="unsend",
    )(x)


def per_device(samples, quantity, variance, grid_point, sort, tab):
    count = lax.axis_size("space")
    space = lax.axis_index("space")
    member = lax.axis_index("member")
    pairs = [[i, i + 1] for i in range(0, count, 2)]
    swap = [(i, i ^ 1) for i in range(count)]
    hop = [(i, (i + (1 if i % 2 else -1)) % count) for i in range(count)]
    odd = space % 2
    at = jnp.stack([member * CELLS, 1 - 2 * odd, 1 - odd]).astype(jnp.int32)

    send, picks, par = pick(samples, quantity, variance, grid_point, sort, tab)
    gathered = lax.all_gather(picks, "member", axis=0).reshape(2 * ROWS, 128)
    own, second = make_bundle(gathered, par)
    off = lax.ppermute(own, "space", hop)
    side = lax.all_gather(own, "space", axis_index_groups=pairs)
    send, side = lax.optimization_barrier((send, side))
    cells = lax.all_to_all(send.reshape(16, 40, 128), "member", 0, 0, tiled=True).reshape(ROWS, 128)
    own2 = replay(replay_kernel, 3, "replay", at, par, second, own, side, off)
    off2 = lax.ppermute(own2, "space", hop)
    side2 = lax.ppermute(own2, "space", swap)[None]
    cells = update(False, at, cells, own, side, off)
    cells = update(True, at, cells, own2, side2, off2)
    back = lax.all_to_all(cells.reshape(16, 40, 128), "member", 0, 0, tiled=True)
    return unsend(back.reshape(ROWS, 128))


def solution(mesh):
    in_specs = (
        P("member", "space"),
        P(None, "space"),
        P(None, "space"),
        P(None, "space"),
        P(None, "space"),
        P(),
    )
    return jax.shard_map(
        per_device, mesh=mesh, in_specs=in_specs, out_specs=P("member", "space"), check_vma=False
    )
```

time: 124 us -> 118 us (0.952); the launches traced: 122 us -> 118 us
  blocking collectives: 79 us -> 71.1 us
  waiting for transfers between devices: 0.01 us -> 7.54 us
  Pallas kernels: 29.4 us -> 25.6 us
  starting transfers between devices: 10.9 us -> 13.2 us
  local copies, waits for them, and re-layouts: 2.13 us -> 0.01 us
    all_to_all x1, waiting for transfers between devices: 0.01 us -> 7.54 us  [per_device(): lax.all_to_all(send.reshape(16, 40, 128), 'member', 0, 0, tiled=True)]
    all_to_all x1, blocking collectives: 33.4 us -> 27.9 us  [per_device(): lax.all_to_all(cells.reshape(16, 40, 128), 'member', 0, 0, tiled=True)]
    pallas_call x5 -> x4, Pallas kernels: 25.2 us -> 21.7 us  [the longest x2 12.5 us: update(): pl.pallas_call(kernel, out_shape=jax.ShapeDtypeStruct((ROWS, 128) if last...]
    all_gather x1 -> x0, blocking collectives: 2.85 us -> none  [per_device(): side2 = lax.all_gather(own2, 'space', axis_index_groups=pairs)]
    ppermute x0 -> x1, starting transfers between devices: none -> 1.99 us  [per_device(): side2 = lax.ppermute(own2, 'space', swap)[None]]
  transfers between devices with their start and end apart: 3 -> 4, of which waited for: 0 -> 1; matrix products, arithmetic and copies ran while one was open for 1% -> 0% of each run, Pallas kernels for 14% -> 13%
where the time goes in v2:
time: 118 us
  blocking collectives  71.1 us (60%)
  Pallas kernels  25.6 us (22%)
  starting transfers between devices  13.2 us (11%)
  waiting for transfers between devices  7.54 us (6%)
    all_gather x1, blocking collectives, per_device(): gathered = lax.all_gather(picks, 'member', axis=0).reshape(2 * ROWS, 128)  40 us
    all_to_all x1, blocking collectives, per_device(): lax.all_to_all(cells.reshape(16, 40, 128), 'member', 0, 0, tiled=True)  27.9 us
    pallas_call x2, Pallas kernels, update(): pl.pallas_call(kernel, out_shape=jax.ShapeDtypeStruct((ROWS, 128) if last...  12.5 us
    pallas_call x1, Pallas kernels, replay(): pl.pallas_call(kernel, out_shape=jax.ShapeDtypeStruct((BUNDLE, CELLS), f3...  9.01 us
    all_to_all x1, waiting for transfers between devices, per_device(): lax.all_to_all(send.reshape(16, 40, 128), 'member', 0, 0, tiled=True)  7.54 us
    all_to_all x1, starting transfers between devices, per_device(): lax.all_to_all(send.reshape(16, 40, 128), 'member', 0, 0, tiled=True)  6.32 us
    all_gather x1, blocking collectives, per_device(): side = lax.all_gather(own, 'space', axis_index_groups=pairs)  3.25 us
    pallas_call x1, Pallas kernels, pick(): pl.pallas_call(pick_kernel, out_shape=(jax.ShapeDtypeStruct((ROWS, 128),...  2.94 us
  transfers between devices with their start and end apart: 4, of which 1 were waited for; matrix products, arithmetic and copies ran while one was open for 0% of the time, Pallas kernels for 13%

profile of v2, /device:TPU:24, one launch (start us, length us, event | category | flops | bytes accessed | tf_op | source)
XLA Modules:
  0.0 117.6 jit_solution(13065568259515077609)
XLA Ops:
  0.0 2.9 %pick.1 = (f32[640,128]{1,0:T(8,128)}, f32[80,128]{1,0:T(8,128)}, f32[32,1024]{1,0:T(8,128)}) custom-call(f32[5,16384]{1,0:T(8,128)} %x_hbm.1, f32[2,1024]{1,0:T(2,128)} %value_hbm.1, f32[2,1024]{1,0:T(2,128)} %error_hbm.1, s32[2,1024]{1,0:T(2,128)} %gp_hbm.1, s32[2,1024]{1,0:T(2,128)} %sort_hbm.1, f32[4,8]{1,0:T(4,128)} %tab_hbm.1), custom_call_target="tpu_custom_call" | custom-call | tf_op jit(solution)/shard_map/pick/pallas_call | solution.py:89
  2.9 0.0 copy-start
  3.0 40.0 %all-gather.gathered_ref = f32[1280,128]{1,0:T(8,128)S(1)} all-gather(f32[80,128]{1,0:T(8,128)} %get-tuple-element.13), channel_id=2, replica_groups=mesh['member'=16,'space'=32] {'member'}, dimensions={0}, use_global_device_ids=true | all-gather | bytes 696320 | tf_op jit(solution)/shard_map/all_gather | solution.py:374
  42.9 0.0 copy-done
  42.9 0.2 bundle.1
  43.1 1.9 %collective-permute-start = (f32[96,1024]{1,0:T(8,128)S(1)}, f32[96,1024]{1,0:T(8,128)S(1)}, u32[]{:S(2)}, u32[]{:S(2)}) collective-permute-start(f32[96,1024]{1,0:T(8,128)S(1)} %get-tuple-element.15.refs_2_.own_ref), channel_id=1, source_target_pairs={{0,31},{1,2},{2,1},{3,4},{4,3},{5,6},{6,5},{7,8},{8,7},{9,10},{10,... | collective-permute-start | bytes 1179656 | tf_op jit(solution)/shard_map/ppermute | solution.py:376
  45.0 3.2 %all-gather.1 = f32[192,1024]{1,0:T(8,128)S(1)} all-gather(f32[96,1024]{1,0:T(8,128)S(1)} %get-tuple-element.15.refs_2_.own_ref), channel_id=3, replica_groups={{0,1},{2,3},{4,5},{6,7},{8,9},{10,11},{12,13},{14,15},{16,17},{18,19},{..., dimensions={0}, use_global_device_ids=true | all-gather | bytes 1179648 | tf_op jit(solution)/shard_map/all_gather | solution.py:377
  48.3 6.3 %all-to-all-start = ((f32[16,40,128]{2,1,0:T(8,128)}), f32[16,40,128]{2,1,0:T(8,128)S(1)}, u32[]{:S(2)}, u32[]{:S(2)}) async-start(f32[16,40,128]{2,1,0:T(8,128)} %bitcast.4), calls=%async_computation | async-start | bytes 655360 | tf_op jit(solution)/shard_map/all_to_all | solution.py:379
  54.6 0.1 pad_add_fusion.refs_0_.at_ref
  54.7 0.0 collective-permute-done.refs_4_.off_ref
  54.7 9.0 %replay.1.refs_2_ = f32[96,1024]{1,0:T(8,128)S(1)} custom-call(s32[3]{0:T(128)S(1)} %pad_add_fusion.refs_0_.at_ref, f32[32,1024]{1,0:T(8,128)S(1)} %copy-done, f32[80,1024]{1,0:T(8,128)S(1)} %get-tuple-element.18.x_ref, f32[96,1024]{1,0:T(8,128)S(1)} %get-tuple-element.15.refs_2_.own_ref, f32[2,96,1024]{2,1,0:T(8,128)S(1)} %bitcast.10, ...), custom_call_target="tpu_custom_call" | custom-call | flops 12000000000 | bytes 2000000 | tf_op jit(solution)/shard_map/replay/pallas_call | solution.py:258
  63.7 2.0 %collective-permute-start.1 = (f32[96,1024]{1,0:T(8,128)S(1)}, f32[96,1024]{1,0:T(8,128)S(1)}, u32[]{:S(2)}, u32[]{:S(2)}) collective-permute-start(f32[96,1024]{1,0:T(8,128)S(1)} %replay.1.refs_2_), channel_id=1, source_target_pairs={{0,1},{1,0},{2,3},{3,2},{4,5},{5,4},{6,7},{7,6},{8,9},{9,8},{10,11... | collective-permute-start | bytes 1179656 | tf_op jit(solution)/shard_map/ppermute | solution.py:382
  65.7 2.9 %collective-permute-start.2 = (f32[96,1024]{1,0:T(8,128)S(1)}, f32[96,1024]{1,0:T(8,128)S(1)}, u32[]{:S(2)}, u32[]{:S(2)}) collective-permute-start(f32[96,1024]{1,0:T(8,128)S(1)} %replay.1.refs_2_), channel_id=1, source_target_pairs={{0,31},{1,2},{2,1},{3,4},{4,3},{5,6},{6,5},{7,8},{8,7},{9,10},{10,... | collective-permute-start | bytes 1179656 | tf_op jit(solution)/shard_map/ppermute | solution.py:381
  68.7 7.5 %all-to-all-done = f32[16,40,128]{2,1,0:T(8,128)S(1)} async-done(((f32[16,40,128]{2,1,0:T(8,128)}), f32[16,40,128]{2,1,0:T(8,128)S(1)}, u32[]{:S(2)}, u32[]{:S(2)}) %all-to-all-start) | async-done | bytes 327712 | tf_op jit(solution)/shard_map/all_to_all | solution.py:379
  76.2 6.3 %update_first.1.refs_1_ = f32[80,1024]{1,0:T(8,128)S(1)} custom-call(s32[3]{0:T(128)S(1)} %pad_add_fusion.refs_0_.at_ref, f32[640,128]{1,0:T(8,128)S(1)} %bitcast.12, f32[96,1024]{1,0:T(8,128)S(1)} %get-tuple-element.15.refs_2_.own_ref, f32[2,96,1024]{2,1,0:T(8,128)S(1)} %bitcast.11, f32[96,1024]{1,0:T(8,128)S(1)} %collective-permute-done.refs_4_.off_ref), custom_call_target="tpu_custom_call" | custom-call | flops 8999999488 | bytes 2000000 | tf_op jit(solution)/shard_map/update_first/pallas_call | solution.py:327
  82.5 0.0 collective-permute-done.1
  82.5 0.0 collective-permute-done.2.refs_4_
  82.5 6.3 %update_last.1 = f32[640,128]{1,0:T(8,128)S(1)} custom-call(s32[3]{0:T(128)S(1)} %pad_add_fusion.refs_0_.at_ref, f32[80,1024]{1,0:T(8,128)S(1)} %update_first.1.refs_1_, f32[96,1024]{1,0:T(8,128)S(1)} %replay.1.refs_2_, f32[1,96,1024]{2,1,0:T(8,128)S(1)} %bitcast.14, f32[96,1024]{1,0:T(8,128)S(1)} %collective-permute-done.2.refs_4_), custom_call_target="tpu_custom_call" | custom-call | flops 8999999488 | bytes 2000000 | tf_op jit(solution)/shard_map/update_last/pallas_call | solution.py:327
  88.8 27.9 %all_to_all.10 = f32[16,40,128]{2,1,0:T(8,128)S(1)} all-to-all(f32[16,40,128]{2,1,0:T(8,128)S(1)} %bitcast.13), channel_id=1, replica_groups=mesh['member'=16,'space'=32] {'member'}, dimensions={0} | all-to-all | bytes 655360 | tf_op jit(solution)/shard_map/all_to_all | solution.py:385
  116.7 0.9 unsend.1
Async XLA Ops:
  2.9 40.0 %copy-start = (f32[32,1024]{1,0:T(8,128)S(1)}, f32[32,1024]{1,0:T(8,128)}, u32[]{:S(2)}) copy-start(f32[32,1024]{1,0:T(8,128)} %get-tuple-element.14.par_ref) | copy-start | bytes 393220
  43.1 11.6 %collective-permute-start = (f32[96,1024]{1,0:T(8,128)S(1)}, f32[96,1024]{1,0:T(8,128)S(1)}, u32[]{:S(2)}, u32[]{:S(2)}) collective-permute-start(f32[96,1024]{1,0:T(8,128)S(1)} %get-tuple-element.15.refs_2_.own_ref), channel_id=1, source_target_pairs={{0,31},{1,2},{2,1},{3,4},{4,3},{5,6},{6,5},{7,8},{8,7},{9,10},{10,... | collective-permute-start | bytes 1179656 | tf_op jit(solution)/shard_map/ppermute | solution.py:376
  48.3 27.9 %all-to-all-start = ((f32[16,40,128]{2,1,0:T(8,128)}), f32[16,40,128]{2,1,0:T(8,128)S(1)}, u32[]{:S(2)}, u32[]{:S(2)}) async-start(f32[16,40,128]{2,1,0:T(8,128)} %bitcast.4), calls=%async_computation | async-start | bytes 655360 | tf_op jit(solution)/shard_map/all_to_all | solution.py:379
  63.7 18.8 %collective-permute-start.1 = (f32[96,1024]{1,0:T(8,128)S(1)}, f32[96,1024]{1,0:T(8,128)S(1)}, u32[]{:S(2)}, u32[]{:S(2)}) collective-permute-start(f32[96,1024]{1,0:T(8,128)S(1)} %replay.1.refs_2_), channel_id=1, source_target_pairs={{0,1},{1,0},{2,3},{3,2},{4,5},{5,4},{6,7},{7,6},{8,9},{9,8},{10,11... | collective-permute-start | bytes 1179656 | tf_op jit(solution)/shard_map/ppermute | solution.py:382
  65.7 16.8 %collective-permute-start.2 = (f32[96,1024]{1,0:T(8,128)S(1)}, f32[96,1024]{1,0:T(8,128)S(1)}, u32[]{:S(2)}, u32[]{:S(2)}) collective-permute-start(f32[96,1024]{1,0:T(8,128)S(1)} %replay.1.refs_2_), channel_id=1, source_target_pairs={{0,31},{1,2},{2,1},{3,4},{4,3},{5,6},{6,5},{7,8},{8,7},{9,10},{10,... | collective-permute-start | bytes 1179656 | tf_op jit(solution)/shard_map/ppermute | solution.py:381

commit v3 on v2

--- a/solution.py
+++ b/solution.py
@@ -241,7 +241,7 @@
     work = (e3_ref, posb_ref, d3_ref, a2_ref, rows_ref, place_ref, acc_ref)
     sections = (
         (own_ref, lambda place: place * sign),
-        (side_ref.at[at_ref[2]], lambda place: place * sign + BLOCK),
+        (side_ref, lambda place: place * sign + BLOCK),
         (off_ref, lambda place: place * sign - BLOCK),
     )
     for sec, (ref, shifted) in enumerate(sections):
@@ -296,7 +296,7 @@
         for r in range(8):
             x_ref[:, r * 128 : (r + 1) * 128] = cells_ref[pl.ds(r, MEMBERS, stride=8), :]
     prepare_cells(x_ref, e3_ref)
-    sections = ((own_ref, start), (side_ref.at[0 if last else at_ref[2]], start - sign * BLOCK), (off_ref, start + sign * BLOCK))
+    sections = ((own_ref, start), (side_ref, start - sign * BLOCK), (off_ref, start + sign * BLOCK))
     for sec, (ref, first) in enumerate(sections):
         prepare_section(sec, ref, d3_ref, a2_ref, rows_ref, start=first)
     acc_ref[...] = jnp.zeros_like(acc_ref)
@@ -364,22 +364,21 @@
     count = lax.axis_size("space")
     space = lax.axis_index("space")
     member = lax.axis_index("member")
-    pairs = [[i, i + 1] for i in range(0, count, 2)]
     swap = [(i, i ^ 1) for i in range(count)]
     hop = [(i, (i + (1 if i % 2 else -1)) % count) for i in range(count)]
     odd = space % 2
-    at = jnp.stack([member * CELLS, 1 - 2 * odd, 1 - odd]).astype(jnp.int32)
+    at = jnp.stack([member * CELLS, 1 - 2 * odd]).astype(jnp.int32)
 
     send, picks, par = pick(samples, quantity, variance, grid_point, sort, tab)
     gathered = lax.all_gather(picks, "member", axis=0).reshape(2 * ROWS, 128)
     own, second = make_bundle(gathered, par)
+    send, own = lax.optimization_barrier((send, own))
+    cells = lax.all_to_all(send.reshape(16, 40, 128), "member", 0, 0, tiled=True).reshape(ROWS, 128)
     off = lax.ppermute(own, "space", hop)
-    side = lax.all_gather(own, "space", axis_index_groups=pairs)
-    send, side = lax.optimization_barrier((send, side))
-    cells = lax.all_to_all(send.reshape(16, 40, 128), "member", 0, 0, tiled=True).reshape(ROWS, 128)
+    side = lax.ppermute(own, "space", swap)
     own2 = replay(replay_kernel, 3, "replay", at, par, second, own, side, off)
     off2 = lax.ppermute(own2, "space", hop)
-    side2 = lax.ppermute(own2, "space", swap)[None]
+    side2 = lax.ppermute(own2, "space", swap)
     cells = update(False, at, cells, own, side, off)
     cells = update(True, at, cells, own2, side2, off2)
     back = lax.all_to_all(cells.reshape(16, 40, 128), "member", 0, 0, tiled=True)

time: 118 us -> 117 us (level)
  blocking collectives: 71.1 us -> 66.6 us
  starting transfers between devices: 13.2 us -> 17 us
    ppermute x1 -> x2, starting transfers between devices: 1.99 us -> 6.76 us  [the longest x1 3.59 us: per_device(): side2 = lax.ppermute(own2, 'space', swap)]
    all_gather x1 -> x0, blocking collectives: 3.25 us -> none  [per_device(): side = lax.all_gather(own, 'space', axis_index_groups=pairs)]
    all_to_all x1, blocking collectives: 27.9 us -> 26.6 us  [per_device(): lax.all_to_all(cells.reshape(16, 40, 128), 'member', 0, 0, tiled=True)]
  transfers between devices with their start and end apart: 4 -> 5, of which waited for: 1 -> 1; matrix products, arithmetic and copies ran while one was open for 0% -> 0% of each run, Pallas kernels for 13% -> 13%
where the time goes in v3:
time: 117 us; the launch traced here: 116 us
  blocking collectives  66.6 us (57%)
  Pallas kernels  25.5 us (22%)
  starting transfers between devices  17 us (15%)
  waiting for transfers between devices  6.41 us (5%)
    all_gather x1, blocking collectives, per_device(): gathered = lax.all_gather(picks, 'member', axis=0).reshape(2 * ROWS, 128)  40 us
    all_to_all x1, blocking collectives, per_device(): lax.all_to_all(cells.reshape(16, 40, 128), 'member', 0, 0, tiled=True)  26.6 us
    pallas_call x2, Pallas kernels, update(): pl.pallas_call(kernel, out_shape=jax.ShapeDtypeStruct((ROWS, 128) if last...  12.5 us
    pallas_call x1, Pallas kernels, replay(): pl.pallas_call(kernel, out_shape=jax.ShapeDtypeStruct((BUNDLE, CELLS), f3...  8.99 us
    all_to_all x1, waiting for transfers between devices, per_device(): lax.all_to_all(send.reshape(16, 40, 128), 'member', 0, 0, tiled=True)  6.4 us
    all_to_all x1, starting transfers between devices, per_device(): lax.all_to_all(send.reshape(16, 40, 128), 'member', 0, 0, tiled=True)  6.31 us
    ppermute x1, starting transfers between devices, per_device(): side2 = lax.ppermute(own2, 'space', swap)  3.59 us
    ppermute x1, starting transfers between devices, per_device(): side = lax.ppermute(own, 'space', swap)  3.16 us
  transfers between devices with their start and end apart: 5, of which 1 were waited for; matrix products, arithmetic and copies ran while one was open for 0% of the time, Pallas kernels for 13%

profile of v3, /device:TPU:24, one launch (start us, length us, event | category | flops | bytes accessed | tf_op | source)
XLA Modules:
  0.0 115.7 jit_solution(8958429873907955179)
XLA Ops:
  0.0 2.9 %pick.1 = (f32[640,128]{1,0:T(8,128)}, f32[80,128]{1,0:T(8,128)}, f32[32,1024]{1,0:T(8,128)}) custom-call(f32[5,16384]{1,0:T(8,128)} %x_hbm.1, f32[2,1024]{1,0:T(2,128)} %value_hbm.1, f32[2,1024]{1,0:T(2,128)} %error_hbm.1, s32[2,1024]{1,0:T(2,128)} %gp_hbm.1, s32[2,1024]{1,0:T(2,128)} %sort_hbm.1, f32[4,8]{1,0:T(4,128)} %tab_hbm.1), custom_call_target="tpu_custom_call" | custom-call | tf_op jit(solution)/shard_map/pick/pallas_call | solution.py:89
  2.9 0.0 copy-start
  3.0 40.0 %all-gather.gathered_ref = f32[1280,128]{1,0:T(8,128)S(1)} all-gather(f32[80,128]{1,0:T(8,128)} %get-tuple-element.13), channel_id=2, replica_groups=mesh['member'=16,'space'=32] {'member'}, dimensions={0}, use_global_device_ids=true | all-gather | bytes 696320 | tf_op jit(solution)/shard_map/all_gather | solution.py:373
  42.9 0.0 copy-done
  42.9 0.2 bundle.1
  43.1 1.9 %collective-permute-start.1 = (f32[96,1024]{1,0:T(8,128)S(1)}, f32[96,1024]{1,0:T(8,128)S(1)}, u32[]{:S(2)}, u32[]{:S(2)}) collective-permute-start(f32[96,1024]{1,0:T(8,128)S(1)} %get-tuple-element.17.refs_2_.own_ref), channel_id=1, source_target_pairs={{0,31},{1,2},{2,1},{3,4},{4,3},{5,6},{6,5},{7,8},{8,7},{9,10},{10,... | collective-permute-start | bytes 1179656 | tf_op jit(solution)/shard_map/ppermute | solution.py:377
  45.0 3.2 %collective-permute-start = (f32[96,1024]{1,0:T(8,128)S(1)}, f32[96,1024]{1,0:T(8,128)S(1)}, u32[]{:S(2)}, u32[]{:S(2)}) collective-permute-start(f32[96,1024]{1,0:T(8,128)S(1)} %get-tuple-element.17.refs_2_.own_ref), channel_id=1, source_target_pairs={{0,1},{1,0},{2,3},{3,2},{4,5},{5,4},{6,7},{7,6},{8,9},{9,8},{10,11... | collective-permute-start | bytes 1179656 | tf_op jit(solution)/shard_map/ppermute | solution.py:378
  48.2 6.3 %all-to-all-start = ((f32[16,40,128]{2,1,0:T(8,128)}), f32[16,40,128]{2,1,0:T(8,128)S(1)}, u32[]{:S(2)}, u32[]{:S(2)}) async-start(f32[16,40,128]{2,1,0:T(8,128)} %bitcast.2), calls=%async_computation | async-start | bytes 655360 | tf_op jit(solution)/shard_map/all_to_all | solution.py:376
  54.5 0.1 pad_add_fusion.refs_0_.at_ref
  54.6 0.0 collective-permute-done.1.refs_4_.off_ref
  54.6 0.0 collective-permute-done.refs_3_.side_ref
  54.6 9.0 %replay.1.refs_2_ = f32[96,1024]{1,0:T(8,128)S(1)} custom-call(s32[2]{0:T(128)S(1)} %pad_add_fusion.refs_0_.at_ref, f32[32,1024]{1,0:T(8,128)S(1)} %copy-done, f32[80,1024]{1,0:T(8,128)S(1)} %get-tuple-element.18.x_ref, f32[96,1024]{1,0:T(8,128)S(1)} %get-tuple-element.17.refs_2_.own_ref, f32[96,1024]{1,0:T(8,128)S(1)} %collective-permute-done.refs_3_.side_ref, ...), custom_call_target="tpu_custom_call" | custom-call | flops 12000000000 | bytes 2000000 | tf_op jit(solution)/shard_map/replay/pallas_call | solution.py:258
  63.6 2.1 %collective-permute-start.3 = (f32[96,1024]{1,0:T(8,128)S(1)}, f32[96,1024]{1,0:T(8,128)S(1)}, u32[]{:S(2)}, u32[]{:S(2)}) collective-permute-start(f32[96,1024]{1,0:T(8,128)S(1)} %replay.1.refs_2_), channel_id=1, source_target_pairs={{0,31},{1,2},{2,1},{3,4},{4,3},{5,6},{6,5},{7,8},{8,7},{9,10},{10,... | collective-permute-start | bytes 1179656 | tf_op jit(solution)/shard_map/ppermute | solution.py:380
  65.7 3.6 %collective-permute-start.2 = (f32[96,1024]{1,0:T(8,128)S(1)}, f32[96,1024]{1,0:T(8,128)S(1)}, u32[]{:S(2)}, u32[]{:S(2)}) collective-permute-start(f32[96,1024]{1,0:T(8,128)S(1)} %replay.1.refs_2_), channel_id=1, source_target_pairs={{0,1},{1,0},{2,3},{3,2},{4,5},{5,4},{6,7},{7,6},{8,9},{9,8},{10,11... | collective-permute-start | bytes 1179656 | tf_op jit(solution)/shard_map/ppermute | solution.py:381
  69.3 6.4 %all-to-all-done = f32[16,40,128]{2,1,0:T(8,128)S(1)} async-done(((f32[16,40,128]{2,1,0:T(8,128)}), f32[16,40,128]{2,1,0:T(8,128)S(1)}, u32[]{:S(2)}, u32[]{:S(2)}) %all-to-all-start) | async-done | bytes 327712 | tf_op jit(solution)/shard_map/all_to_all | solution.py:376
  75.7 6.3 %update_first.1.refs_1_ = f32[80,1024]{1,0:T(8,128)S(1)} custom-call(s32[2]{0:T(128)S(1)} %pad_add_fusion.refs_0_.at_ref, f32[640,128]{1,0:T(8,128)S(1)} %bitcast.7, f32[96,1024]{1,0:T(8,128)S(1)} %get-tuple-element.17.refs_2_.own_ref, f32[96,1024]{1,0:T(8,128)S(1)} %collective-permute-done.refs_3_.side_ref, ...), custom_call_target="tpu_custom_call" | custom-call | flops 8999999488 | bytes 2000000 | tf_op jit(solution)/shard_map/update_first/pallas_call | solution.py:327
  82.0 0.0 collective-permute-done.3.refs_4_
  82.0 0.0 collective-permute-done.2.refs_3_
  82.0 6.2 %update_last.1 = f32[640,128]{1,0:T(8,128)S(1)} custom-call(s32[2]{0:T(128)S(1)} %pad_add_fusion.refs_0_.at_ref, f32[80,1024]{1,0:T(8,128)S(1)} %update_first.1.refs_1_, f32[96,1024]{1,0:T(8,128)S(1)} %replay.1.refs_2_, f32[96,1024]{1,0:T(8,128)S(1)} %collective-permute-done.2.refs_3_, f32[96,1024]{1,0:T(8,128)S(1)} %collective-permute-done.3.refs_4_), custom_call_target="tpu_custom_call" | custom-call | flops 8999999488 | bytes 2000000 | tf_op jit(solution)/shard_map/update_last/pallas_call | solution.py:327
  88.2 26.6 %all_to_all.10 = f32[16,40,128]{2,1,0:T(8,128)S(1)} all-to-all(f32[16,40,128]{2,1,0:T(8,128)S(1)} %bitcast.8), channel_id=1, replica_groups=mesh['member'=16,'space'=32] {'member'}, dimensions={0} | all-to-all | bytes 655360 | tf_op jit(solution)/shard_map/all_to_all | solution.py:384
  114.8 0.9 unsend.1
Async XLA Ops:
  2.9 40.0 %copy-start = (f32[32,1024]{1,0:T(8,128)S(1)}, f32[32,1024]{1,0:T(8,128)}, u32[]{:S(2)}) copy-start(f32[32,1024]{1,0:T(8,128)} %get-tuple-element.14.par_ref) | copy-start | bytes 393220
  43.1 11.5 %collective-permute-start.1 = (f32[96,1024]{1,0:T(8,128)S(1)}, f32[96,1024]{1,0:T(8,128)S(1)}, u32[]{:S(2)}, u32[]{:S(2)}) collective-permute-start(f32[96,1024]{1,0:T(8,128)S(1)} %get-tuple-element.17.refs_2_.own_ref), channel_id=1, source_target_pairs={{0,31},{1,2},{2,1},{3,4},{4,3},{5,6},{6,5},{7,8},{8,7},{9,10},{10,... | collective-permute-start | bytes 1179656 | tf_op jit(solution)/shard_map/ppermute | solution.py:377
  45.0 9.6 %collective-permute-start = (f32[96,1024]{1,0:T(8,128)S(1)}, f32[96,1024]{1,0:T(8,128)S(1)}, u32[]{:S(2)}, u32[]{:S(2)}) collective-permute-start(f32[96,1024]{1,0:T(8,128)S(1)} %get-tuple-element.17.refs_2_.own_ref), channel_id=1, source_target_pairs={{0,1},{1,0},{2,3},{3,2},{4,5},{5,4},{6,7},{7,6},{8,9},{9,8},{10,11... | collective-permute-start | bytes 1179656 | tf_op jit(solution)/shard_map/ppermute | solution.py:378
  48.2 27.5 %all-to-all-start = ((f32[16,40,128]{2,1,0:T(8,128)}), f32[16,40,128]{2,1,0:T(8,128)S(1)}, u32[]{:S(2)}, u32[]{:S(2)}) async-start(f32[16,40,128]{2,1,0:T(8,128)} %bitcast.2), calls=%async_computation | async-start | bytes 655360 | tf_op jit(solution)/shard_map/all_to_all | solution.py:376
  63.6 18.3 %collective-permute-start.3 = (f32[96,1024]{1,0:T(8,128)S(1)}, f32[96,1024]{1,0:T(8,128)S(1)}, u32[]{:S(2)}, u32[]{:S(2)}) collective-permute-start(f32[96,1024]{1,0:T(8,128)S(1)} %replay.1.refs_2_), channel_id=1, source_target_pairs={{0,31},{1,2},{2,1},{3,4},{4,3},{5,6},{6,5},{7,8},{8,7},{9,10},{10,... | collective-permute-start | bytes 1179656 | tf_op jit(solution)/shard_map/ppermute | solution.py:380
  65.7 16.3 %collective-permute-start.2 = (f32[96,1024]{1,0:T(8,128)S(1)}, f32[96,1024]{1,0:T(8,128)S(1)}, u32[]{:S(2)}, u32[]{:S(2)}) collective-permute-start(f32[96,1024]{1,0:T(8,128)S(1)} %replay.1.refs_2_), channel_id=1, source_target_pairs={{0,1},{1,0},{2,3},{3,2},{4,5},{5,4},{6,7},{7,6},{8,9},{9,8},{10,11... | collective-permute-start | bytes 1179656 | tf_op jit(solution)/shard_map/ppermute | solution.py:381
